TPU v7x, 32 devices: a whole 2x2x4 slice. The times are simulated.
32 devices in a mesh: fsdp: 8 (over z, core), ctx: 2 (over y), tp: 2 (over x).
Axes of the slice: x: 2, y: 2, z: 4, core: 2. Of those that a mesh axis runs over, the one named last changes fastest.
Arguments:
- hidden_in: bfloat16 [8, 1024, 1024], P('fsdp', 'ctx'), may hold values from -6 to 6
- segment_ids: int32 [8, 1024], P('fsdp'), may hold values from 0 to 4, as said below
- expert_ids: int32 [8, 1024, 8], P('fsdp', 'ctx'), may hold values from 0 to 31, all different within a row; in each aligned block of 512 rows (0 to 511, 512 to 1023, ..., all dimensions but the last counted through in order) at most 256 rows name the same one
- norm1_gain: bfloat16 [1024], P('fsdp'), may hold values from 0.5 to 1.5
- w_query: bfloat16 [1024, 1024], P('fsdp', 'tp'), may hold values from -0.1875 to 0.1875
- w_key: bfloat16 [1024, 512], P('fsdp', 'tp'), may hold values from -0.1875 to 0.1875
- w_value: bfloat16 [1024, 512], P('fsdp', 'tp'), may hold values from -0.1875 to 0.1875
- w_output: bfloat16 [1024, 1024], P('tp', 'fsdp'), may hold values from -1.5 to 1.5
- norm2_gain: bfloat16 [1024], P('fsdp'), may hold values from 0.5 to 1.5
- w_router: bfloat16 [1024, 32], P('fsdp'), may hold values from -0.09375 to 0.09375
- w_gate: bfloat16 [32, 1024, 512], P(None, 'fsdp', 'tp'), may hold values from -0.1875 to 0.1875
- w_up: bfloat16 [32, 1024, 512], P(None, 'fsdp', 'tp'), may hold values from -0.1875 to 0.1875
- w_down: bfloat16 [32, 512, 1024], P(None, 'tp', 'fsdp'), may hold values from -3 to 3
- cotangent: bfloat16 [8, 1024, 1024], P('fsdp', 'ctx'), may hold values from -6 to 6
Outputs:
- block_out: bfloat16 [8, 1024, 1024], P('fsdp', 'ctx')
- grad_hidden_in: float32 [8, 1024, 1024], P('fsdp', 'ctx')
- grad_norm1_gain: float32 [1024], P('fsdp')
- grad_w_query: float32 [1024, 1024], P('fsdp', 'tp')
- grad_w_key: float32 [1024, 512], P('fsdp', 'tp')
- grad_w_value: float32 [1024, 512], P('fsdp', 'tp')
- grad_w_output: float32 [1024, 1024], P('tp', 'fsdp')
- grad_norm2_gain: float32 [1024], P('fsdp')
- grad_w_router: float32 [1024, 32], P('fsdp')
- grad_w_gate: float32 [32, 1024, 512], P(None, 'fsdp', 'tp')
- grad_w_up: float32 [32, 1024, 512], P(None, 'fsdp', 'tp')
- grad_w_down: float32 [32, 512, 1024], P(None, 'tp', 'fsdp')
Inputs may be any that keep to these rules, and one draw needn't show every extreme that they name: `segment_ids`: segment numbers never fall along a row and every row holds all five; in each row document 2 begins within the first 512 positions and ends within the last 512. `expert_ids`: A token names 8 different experts. In each aligned block of 512 tokens of a row (one device's positions of one sequence) no expert is named by more than 256 tokens, and in some block one expert is named by exactly 256.
All inputs are finite; a program needn't handle non-finite values.
Results may differ from a plain program's by a relative error of at most 0.02.
Values may be sent and summed in bfloat16 or wider, within the bound.
A program may use at most 384 MiB of HBM per device.

v0:
```python
import jax
import jax.numpy as jnp
from jax import lax
from jax.sharding import PartitionSpec as P

HD = 64
E = 32
TOPK = 8


epsilon = 1e-05
rope_base = 10000.0
masked_fill = -1e30


def matmul(left, right):
    return jnp.dot(left, right, preferred_element_type=jnp.float32)


def contract_rows(left, right):
    return lax.dot_general(
        left, right, (((0,), (0,)), ((), ())), preferred_element_type=jnp.float32
    )


def contract_cols(left, right):
    return lax.dot_general(
        left, right, (((1,), (1,)), ((), ())), preferred_element_type=jnp.float32
    )


def rms_factor(values):
    return lax.rsqrt(jnp.mean(values * values, axis=-1, keepdims=True) + epsilon)


def doc_positions(segments):
    index = lax.broadcasted_iota(jnp.int32, segments.shape, 1)
    earlier = jnp.concatenate([segments[:, :1], segments[:, :-1]], axis=1)
    starts = jnp.where((segments != earlier) | (index == 0), index, 0)
    return index - lax.cummax(starts, axis=1)


def rotary_tables(positions, head_size):
    half_size = head_size // 2
    exponent = jnp.arange(half_size, dtype=jnp.float32) * (-2.0 / head_size)
    angles = positions.astype(jnp.float32)[..., None] * jnp.power(rope_base, exponent)
    return (jnp.cos(angles), jnp.sin(angles))


def rotate(values, cosine, sine_tab):
    half_size = values.shape[-1] // 2
    first_half = values[..., :half_size]
    second_half = values[..., half_size:]
    cos_wide = cosine[..., None, :]
    sin_wide = sine_tab[..., None, :]
    return jnp.concatenate(
        [
            first_half * cos_wide - second_half * sin_wide,
            second_half * cos_wide + first_half * sin_wide,
        ],
        axis=-1,
    )


def norm_backward(grad_normed, normed, factor, gain):
    scaled = grad_normed * gain
    return factor * (scaled - normed * jnp.mean(scaled * normed, axis=-1, keepdims=True))


def expert_forward(slots, gate_w, up_w, down_w):
    gate_pre = jnp.einsum("ecd,edf->ecf", slots, gate_w, preferred_element_type=jnp.float32)
    up_pre = jnp.einsum("ecd,edf->ecf", slots, up_w, preferred_element_type=jnp.float32)
    sigmoid_g = jax.nn.sigmoid(gate_pre)
    activated = gate_pre * sigmoid_g
    hidden = (activated * up_pre).astype(jnp.bfloat16)
    expert_out = jnp.einsum("ecf,efd->ecd", hidden, down_w, preferred_element_type=jnp.float32)
    return (gate_pre, up_pre, sigmoid_g, activated, hidden, expert_out)


def expert_backward(
    slots, grad_slots, gate_pre, up_pre, sigmoid_g, activated, hidden, gate_w, up_w, down_w
):
    grad_down = jnp.einsum("ecf,ecd->efd", hidden, grad_slots, preferred_element_type=jnp.float32)
    grad_hidden = jnp.einsum("ecd,efd->ecf", grad_slots, down_w, preferred_element_type=jnp.float32)
    grad_gate_pre = (
        grad_hidden * up_pre * sigmoid_g * (1.0 + gate_pre * (1.0 - sigmoid_g))
    ).astype(jnp.bfloat16)
    grad_up_pre = (grad_hidden * activated).astype(jnp.bfloat16)
    grad_gate = jnp.einsum("ecd,ecf->edf", slots, grad_gate_pre, preferred_element_type=jnp.float32)
    grad_up = jnp.einsum("ecd,ecf->edf", slots, grad_up_pre, preferred_element_type=jnp.float32)
    grad_rows = jnp.einsum(
        "ecf,edf->ecd", grad_gate_pre, gate_w, preferred_element_type=jnp.float32
    ) + jnp.einsum("ecf,edf->ecd", grad_up_pre, up_w, preferred_element_type=jnp.float32)
    return (grad_down, grad_gate, grad_up, grad_rows)


def body(
    hidden_in,
    segment_ids,
    expert_ids,
    norm1_gain,
    w_query,
    w_key,
    w_value,
    w_output,
    norm2_gain,
    w_router,
    w_gate,
    w_up,
    w_down,
    cotangent,
):
    row_count, ctx_tok, model_width = hidden_in.shape
    tok_count = row_count * ctx_tok
    seq_len = segment_ids.shape[1]
    first_pos = lax.axis_index("ctx") * ctx_tok
    score_scale = HD ** (-0.5)
    gain_one, query_w, key_w, value_w, out_w, gain_two, router_w = (
        lax.all_gather(norm1_gain, "fsdp", axis=0, tiled=True),
        lax.all_gather(w_query, "fsdp", axis=0, tiled=True),
        lax.all_gather(w_key, "fsdp", axis=0, tiled=True),
        lax.all_gather(w_value, "fsdp", axis=0, tiled=True),
        lax.all_gather(w_output, "fsdp", axis=1, tiled=True),
        lax.all_gather(norm2_gain, "fsdp", axis=0, tiled=True),
        lax.all_gather(w_router, "fsdp", axis=0, tiled=True),
    )
    inputs = hidden_in.reshape(tok_count, model_width).astype(jnp.float32)
    factor_one = rms_factor(inputs)
    normed_one = inputs * factor_one
    first_in = (normed_one * gain_one.astype(jnp.float32)).astype(jnp.bfloat16)
    query_lin = matmul(first_in, query_w)
    key_lin = matmul(first_in, key_w)
    values = matmul(first_in, value_w).astype(jnp.bfloat16)
    heads_q = query_lin.shape[1] // HD
    heads_k = key_lin.shape[1] // HD
    group_size = heads_q // heads_k
    positions = doc_positions(segment_ids)
    local_pos = lax.dynamic_slice_in_dim(positions, first_pos, ctx_tok, 1).reshape(tok_count)
    cosine, sine_tab = rotary_tables(local_pos, HD)
    queries = rotate(query_lin.reshape(tok_count, heads_q, HD), cosine, sine_tab).astype(
        jnp.bfloat16
    )
    keys_rot = rotate(key_lin.reshape(tok_count, heads_k, HD), cosine, sine_tab).astype(
        jnp.bfloat16
    )
    keys_all, values_all = (
        lax.all_gather(
            keys_rot.reshape(row_count, ctx_tok, heads_k * HD), "ctx", axis=1, tiled=True
        ),
        lax.all_gather(values.reshape(row_count, ctx_tok, heads_k * HD), "ctx", axis=1, tiled=True),
    )
    pair_count = row_count * heads_k
    query_pairs = (
        queries.reshape(row_count, ctx_tok, heads_k, group_size, HD)
        .transpose(0, 2, 3, 1, 4)
        .reshape(pair_count, group_size * ctx_tok, HD)
    )
    key_pairs = (
        keys_all.reshape(row_count, seq_len, heads_k, HD)
        .transpose(0, 2, 1, 3)
        .reshape(pair_count, seq_len, HD)
    )
    value_pairs = (
        values_all.reshape(row_count, seq_len, heads_k, HD)
        .transpose(0, 2, 1, 3)
        .reshape(pair_count, seq_len, HD)
    )
    row_of = jnp.arange(pair_count, dtype=jnp.int32) // heads_k
    key_index = jnp.arange(seq_len, dtype=jnp.int32)
    query_index = jnp.tile(first_pos + jnp.arange(ctx_tok, dtype=jnp.int32), group_size)

    def pair_scores(query_block, key_block, row_pick):
        seg_row = lax.dynamic_index_in_dim(segment_ids, row_pick, 0, keepdims=False)
        seg_query = jnp.tile(lax.dynamic_slice_in_dim(seg_row, first_pos, ctx_tok), group_size)
        allowed = (key_index[None, :] <= query_index[:, None]) & (
            seg_query[:, None] == seg_row[None, :]
        )
        raw_scores = contract_cols(query_block, key_block) * score_scale
        return jnp.where(allowed, raw_scores, masked_fill)

    def forward_pair(parts_in):
        query_block, key_block, value_block, row_pick = parts_in
        scores = pair_scores(query_block, key_block, row_pick)
        row_max = jnp.max(scores, axis=-1, keepdims=True)
        exp_vals = jnp.exp(scores - row_max)
        totals = jnp.sum(exp_vals, axis=-1, keepdims=True)
        weights_p = (exp_vals / totals).astype(jnp.bfloat16)
        return (matmul(weights_p, value_block), (row_max + jnp.log(totals))[:, 0])

    mixture, log_totals = lax.map(forward_pair, (query_pairs, key_pairs, value_pairs, row_of))
    att_out = (
        mixture.reshape(row_count, heads_k, group_size, ctx_tok, HD)
        .transpose(0, 3, 1, 2, 4)
        .reshape(tok_count, heads_q * HD)
        .astype(jnp.bfloat16)
    )
    resid = inputs + lax.psum(matmul(att_out, out_w), "tp")
    factor_two = rms_factor(resid)
    normed_two = resid * factor_two
    second_in = (normed_two * gain_two.astype(jnp.float32)).astype(jnp.bfloat16)
    logits = matmul(second_in, router_w)
    exp_logits = jnp.exp(logits - jnp.max(logits, axis=-1, keepdims=True))
    router = exp_logits / jnp.sum(exp_logits, axis=-1, keepdims=True)
    route_ids = expert_ids.reshape(tok_count, TOPK)
    chosen = (route_ids[:, :, None] == jnp.arange(E, dtype=jnp.int32)).astype(jnp.float32)
    gate_vals = jnp.sum(chosen * router[:, None, :], axis=-1)
    capacity = tok_count // 2
    flat_ids = route_ids.reshape(-1)
    expert_hits = (flat_ids[:, None] == jnp.arange(E, dtype=jnp.int32)).astype(jnp.int32)
    slot_rank = jnp.sum((jnp.cumsum(expert_hits, axis=0) - expert_hits) * expert_hits, axis=1)
    slot_index = flat_ids * capacity + slot_rank
    token_of = jnp.arange(tok_count * TOPK, dtype=jnp.int32) // TOPK
    buffer = (
        jnp.zeros((E * capacity, model_width), jnp.bfloat16)
        .at[slot_index]
        .set(second_in[token_of])
        .reshape(E, capacity, model_width)
    )
    gate_w, up_w, down_w = (
        lax.all_gather(w_gate, "fsdp", axis=1, tiled=True),
        lax.all_gather(w_up, "fsdp", axis=1, tiled=True),
        lax.all_gather(w_down, "fsdp", axis=2, tiled=True),
    )
    gate_pre, up_pre, sigmoid_g, activated, hidden, expert_out = expert_forward(
        buffer, gate_w, up_w, down_w
    )
    flat_out = expert_out.reshape(E * capacity, model_width)
    routed = flat_out[slot_index].reshape(tok_count, TOPK, model_width)
    moe_total = lax.psum(
        jnp.sum(gate_vals[:, :, None] * routed, axis=1).astype(jnp.bfloat16), "tp"
    ).astype(jnp.float32)
    block_out = (resid + moe_total).astype(jnp.bfloat16).reshape(row_count, ctx_tok, model_width)
    grad_out = cotangent.reshape(tok_count, model_width).astype(jnp.float32)
    spread_grad = grad_out[token_of]
    gate_grad_part = jnp.sum(spread_grad.reshape(tok_count, TOPK, model_width) * routed, axis=-1)
    grad_routed = (gate_vals.reshape(-1)[:, None] * spread_grad).astype(jnp.bfloat16)
    grad_buffer = (
        jnp.zeros((E * capacity, model_width), jnp.bfloat16)
        .at[slot_index]
        .set(grad_routed)
        .reshape(E, capacity, model_width)
    )
    grad_down, grad_gate, grad_up, grad_rows = expert_backward(
        buffer, grad_buffer, gate_pre, up_pre, sigmoid_g, activated, hidden, gate_w, up_w, down_w
    )
    flat_rows = grad_rows.reshape(E * capacity, model_width)
    grad_in_part = jnp.sum(flat_rows[slot_index].reshape(tok_count, TOPK, model_width), axis=1)
    grad_in_sum, grad_gates = lax.psum((grad_in_part, gate_grad_part), "tp")
    grad_route = jnp.sum(grad_gates[:, :, None] * chosen, axis=1)
    grad_logits = (
        router * (grad_route - jnp.sum(router * grad_route, axis=-1, keepdims=True))
    ).astype(jnp.bfloat16)
    grad_router = contract_rows(second_in, grad_logits)
    grad_second = grad_in_sum + contract_cols(grad_logits, router_w)
    grad_gain_two = jnp.sum(grad_second * normed_two, axis=0)
    grad_resid = grad_out + norm_backward(
        grad_second, normed_two, factor_two, gain_two.astype(jnp.float32)
    )
    grad_att = grad_resid.astype(jnp.bfloat16)
    grad_out_w = contract_rows(att_out, grad_att)
    grad_att_out = contract_cols(grad_att, out_w).astype(jnp.bfloat16)
    grad_out_pairs = (
        grad_att_out.reshape(row_count, ctx_tok, heads_k, group_size, HD)
        .transpose(0, 2, 3, 1, 4)
        .reshape(pair_count, group_size * ctx_tok, HD)
    )

    def backward_pair(parts_in):
        query_block, key_block, value_block, grad_block, log_row, row_pick = parts_in
        scores = pair_scores(query_block, key_block, row_pick)
        weights_p = jnp.exp(scores - log_row[:, None])
        grad_p = contract_cols(grad_block, value_block)
        grad_v = contract_rows(weights_p.astype(jnp.bfloat16), grad_block)
        grad_s = (
            weights_p * (grad_p - jnp.sum(weights_p * grad_p, axis=-1, keepdims=True))
        ).astype(jnp.bfloat16)
        grad_q = matmul(grad_s, key_block) * score_scale
        grad_k = contract_rows(grad_s, query_block) * score_scale
        return (grad_q, grad_k, grad_v)

    grad_q_pairs, grad_k_pairs, grad_v_pairs = lax.map(
        backward_pair, (query_pairs, key_pairs, value_pairs, grad_out_pairs, log_totals, row_of)
    )
    grad_k_rows = (
        grad_k_pairs.reshape(row_count, heads_k, seq_len, HD)
        .transpose(0, 2, 1, 3)
        .reshape(row_count, seq_len, heads_k * HD)
    )
    grad_v_rows = (
        grad_v_pairs.reshape(row_count, heads_k, seq_len, HD)
        .transpose(0, 2, 1, 3)
        .reshape(row_count, seq_len, heads_k * HD)
    )
    own_k, own_v = (
        lax.psum_scatter(grad_k_rows, "ctx", scatter_dimension=1, tiled=True),
        lax.psum_scatter(grad_v_rows, "ctx", scatter_dimension=1, tiled=True),
    )
    grad_q_rot = (
        grad_q_pairs.reshape(row_count, heads_k, group_size, ctx_tok, HD)
        .transpose(0, 3, 1, 2, 4)
        .reshape(tok_count, heads_q, HD)
    )
    grad_query_lin = (
        rotate(grad_q_rot, cosine, -sine_tab).reshape(tok_count, heads_q * HD).astype(jnp.bfloat16)
    )
    grad_key_lin = (
        rotate(own_k.reshape(tok_count, heads_k, HD), cosine, -sine_tab)
        .reshape(tok_count, heads_k * HD)
        .astype(jnp.bfloat16)
    )
    grad_value_lin = own_v.reshape(tok_count, heads_k * HD).astype(jnp.bfloat16)
    grad_query = contract_rows(first_in, grad_query_lin)
    grad_key = contract_rows(first_in, grad_key_lin)
    grad_value = contract_rows(first_in, grad_value_lin)
    grad_first_part = (
        contract_cols(grad_query_lin, query_w)
        + contract_cols(grad_key_lin, key_w)
        + contract_cols(grad_value_lin, value_w)
    )
    grad_first = lax.psum(grad_first_part.astype(jnp.bfloat16), "tp").astype(jnp.float32)
    grad_gain_one = jnp.sum(grad_first * normed_one, axis=0)
    grad_input = grad_resid + norm_backward(
        grad_first, normed_one, factor_one, gain_one.astype(jnp.float32)
    )
    dense = (
        lax.psum_scatter(
            grad_gain_one.astype(jnp.bfloat16), "fsdp", scatter_dimension=0, tiled=True
        ).astype(jnp.float32),
        lax.psum_scatter(
            grad_query.astype(jnp.bfloat16), "fsdp", scatter_dimension=0, tiled=True
        ).astype(jnp.float32),
        lax.psum_scatter(
            grad_key.astype(jnp.bfloat16), "fsdp", scatter_dimension=0, tiled=True
        ).astype(jnp.float32),
        lax.psum_scatter(
            grad_value.astype(jnp.bfloat16), "fsdp", scatter_dimension=0, tiled=True
        ).astype(jnp.float32),
        lax.psum_scatter(
            grad_out_w.astype(jnp.bfloat16), "fsdp", scatter_dimension=1, tiled=True
        ).astype(jnp.float32),
        lax.psum_scatter(
            grad_gain_two.astype(jnp.bfloat16), "fsdp", scatter_dimension=0, tiled=True
        ).astype(jnp.float32),
        lax.psum_scatter(
            grad_router.astype(jnp.bfloat16), "fsdp", scatter_dimension=0, tiled=True
        ).astype(jnp.float32),
    )
    gate_part, up_part, down_part = (
        lax.psum_scatter(
            grad_gate.astype(jnp.bfloat16), "fsdp", scatter_dimension=1, tiled=True
        ).astype(jnp.float32),
        lax.psum_scatter(
            grad_up.astype(jnp.bfloat16), "fsdp", scatter_dimension=1, tiled=True
        ).astype(jnp.float32),
        lax.psum_scatter(
            grad_down.astype(jnp.bfloat16), "fsdp", scatter_dimension=2, tiled=True
        ).astype(jnp.float32),
    )
    totals_all = (
        lax.psum(dense[0].astype(jnp.bfloat16), "ctx").astype(jnp.float32),
        lax.psum(dense[1].astype(jnp.bfloat16), "ctx").astype(jnp.float32),
        lax.psum(dense[2].astype(jnp.bfloat16), "ctx").astype(jnp.float32),
        lax.psum(dense[3].astype(jnp.bfloat16), "ctx").astype(jnp.float32),
        lax.psum(dense[4].astype(jnp.bfloat16), "ctx").astype(jnp.float32),
        lax.psum(dense[5].astype(jnp.bfloat16), "ctx").astype(jnp.float32),
        lax.psum(dense[6].astype(jnp.bfloat16), "ctx").astype(jnp.float32),
        lax.psum(gate_part.astype(jnp.bfloat16), "ctx").astype(jnp.float32),
        lax.psum(up_part.astype(jnp.bfloat16), "ctx").astype(jnp.float32),
        lax.psum(down_part.astype(jnp.bfloat16), "ctx").astype(jnp.float32),
    )
    return (
        block_out,
        grad_input.reshape(row_count, ctx_tok, model_width),
        totals_all[0],
        totals_all[1],
        totals_all[2],
        totals_all[3],
        totals_all[4],
        totals_all[5],
        totals_all[6],
        totals_all[7],
        totals_all[8],
        totals_all[9],
    )


def solution(mesh):
    placed = (
        P("fsdp", "ctx", None),
        P("fsdp", None),
        P("fsdp", "ctx", None),
        P("fsdp"),
        P("fsdp", "tp"),
        P("fsdp", "tp"),
        P("fsdp", "tp"),
        P("tp", "fsdp"),
        P("fsdp"),
        P("fsdp", None),
        P(None, "fsdp", "tp"),
        P(None, "fsdp", "tp"),
        P(None, "tp", "fsdp"),
        P("fsdp", "ctx", None),
    )
    return jax.shard_map(
        body,
        mesh=mesh,
        in_specs=placed,
        out_specs=(
            P("fsdp", "ctx", None),
            P("fsdp", "ctx", None),
            P("fsdp"),
            P("fsdp", "tp"),
            P("fsdp", "tp"),
            P("fsdp", "tp"),
            P("tp", "fsdp"),
            P("fsdp"),
            P("fsdp", None),
            P(None, "fsdp", "tp"),
            P(None, "fsdp", "tp"),
            P(None, "tp", "fsdp"),
        ),
        check_vma=False,
    )
```

profile of v0, /device:TPU:0, one launch (start us, length us, event | category | flops | bytes accessed | tf_op | source)
XLA Modules:
  0.0 1933.4 jit_solution(5786741003728692414)
XLA Ops:
  12.9 13.5 all-gather.1
  28.0 15.6 all_gather.38
  47.4 9.2 all_gather.39
  57.3 14.8 all_gather.40
  73.4 9.2 all-gather
  83.1 2.3 copy.81
  88.5 2.4 copy.82
  90.8 23.3 %while.36 = (s32[]{:T(128)}, bf16[4,1024,64]{1,2,0:T(8,128)(2,1)}, f32[4,1024]{1,0:T(4,128)}, s32[1,512]{1,0:T(1,128)S(1)}, s32[1,1024]{1,0:T(1,128)S(1)}, /*ind...) while((s32[]{:T(128)}, bf16[4,1024,64]{1,2,0:T(8,128)(2,1)}, ...), condition=%wide.region_6.7_spmd.clone.clone, body=%wide.region_3.6_spmd.clone.sunk.clone | while | flops 279968768 | bytes 17909920 | solution.py:190
  96.7 2.1 fusion.193
  102.5 2.1 fusion.193
  108.3 2.1 fusion.193
  114.2 2.6 convert_element_type.273
  118.7 3.4 fusion.114
  124.8 9.2 reduce-window.16
  135.0 9.2 all-gather.2
  145.8 18.6 gather_fusion.1
  164.4 12.9 all_gather.44
  179.1 4.5 all-reduce.11.cloned.1.call-done
  187.1 67.1 %scatter_custom_fusion = bf16[8192,1024]{1,0:T(8,128)(2,1)} fusion(s32[4096]{0:T(1024)S(1)} %bitcast.398, bf16[512,1024]{1,0:T(8,128)(2,1)S(1)} %multiply_convert_fusion.6, s32[4096]{0:T(1024)S(1)} %broadcast_clamp_fusion.1, bf16[]{:T(256)} %constant.177.clone.1), kind=kCustom, calls=%fused_computation.78 | custom fusion | bytes 16777218 | tf_op jit(solution)/shard_map/scatter | solution.py:216
  255.4 80.9 %all-gather.13.cloned.1.call-done = bf16[32,1024,256]{2,1,0:T(8,128)(2,1)} async-done(((bf16[32,128,256]{2,1,0:T(8,128)(2,1)}), bf16[32,1024,256]{2,1,0:T(8,128)(2,1)}) %all-gather.13.cloned.1.call-update) | async-done | bytes 16777232 | tf_op jit(solution)/shard_map/all_gather | solution.py:220
  336.3 17.7 fusion.115
  354.0 133.1 %all-gather.15.cloned.1.call-done = bf16[32,1024,256]{2,1,0:T(8,128)(2,1)} async-done(((bf16[32,128,256]{2,1,0:T(8,128)(2,1)}), bf16[32,1024,256]{2,1,0:T(8,128)(2,1)}) %all-gather.15.cloned.1.call-update) | async-done | bytes 16777232 | tf_op jit(solution)/shard_map/all_gather | solution.py:221
  487.1 22.1 %multiply_convert_fusion.5 = (bf16[32,256,256]{2,1,0:T(8,128)(2,1)}, f32[32,256,256]{2,1,0:T(8,128)}) fusion(f32[32,256,256]{2,1,0:T(8,128)} %fusion.115, bf16[32,256,1024]{2,1,0:T(8,128)(2,1)} %bitcast.350, bf16[32,1024,256]{2,1,0:T(8,128)(2,1)} %all-gather.15.cloned.1.call-done), kind=kOutput, calls=%fused_computation.83 | convolution fusion | flops 4307550208 | bytes 54525952 | tf_op jit(solution)/shard_map/ecd,edf->ecf/dot_general | solution.py:72
  509.2 129.5 %all-gather.17.cloned.1.call-done = bf16[32,256,1024]{2,1,0:T(8,128)(2,1)} async-done(((bf16[32,256,128]{2,1,0:T(8,128)(2,1)}), bf16[32,256,1024]{2,1,0:T(8,128)(2,1)}) %all-gather.17.cloned.1.call-update) | async-done | bytes 16777232 | tf_op jit(solution)/shard_map/all_gather | solution.py:222
  638.7 19.6 %fusion.116 = f32[32,256,1024]{2,1,0:T(8,128)} fusion(bf16[32,256,256]{2,1,0:T(8,128)(2,1)} %get-tuple-element.486, bf16[32,256,1024]{2,1,0:T(8,128)(2,1)} %all-gather.17.cloned.1.call-done), kind=kOutput, calls=%fused_computation.203 | convolution fusion | flops 4294967296 | bytes 54525952 | tf_op jit(solution)/shard_map/ecf,efd->ecd/dot_general | solution.py:76
  658.3 33.0 %gather_fusion = f32[4096,1024]{1,0:T(8,128)} fusion(f32[8192,1024]{1,0:T(8,128)} %bitcast.347, s32[4096]{0:T(1024)S(1)} %broadcast_clamp_fusion), kind=kCustom, calls=%fused_computation.1 | custom fusion | bytes 33570816 | tf_op jit(solution)/shard_map/gather | solution.py:228
  691.2 11.3 multiply_reduce_fusion.1
  702.7 12.1 psum.108
  715.4 30.6 %scatter_custom_fusion.1 = bf16[8192,1024]{1,0:T(8,128)(2,1)} fusion(s32[4096]{0:T(1024)S(1)} %bitcast.399, f32[4096,1024]{1,0:T(8,128)} %gather_fusion.1, f32[4096]{0:T(1024)S(1)} %mul.414, bf16[]{:T(256)} %constant.177.clone.1), kind=kCustom, calls=%fused_computation.77 | custom fusion | flops 8388608 | bytes 33570816 | tf_op jit(solution)/shard_map/scatter | solution.py:240
  746.0 21.8 %multiply_convert_fusion.3 = (bf16[32,256,256]{2,1,0:T(8,128)(2,1)}, bf16[32,256,256]{2,1,0:T(8,128)(2,1)}) fusion(f32[32,256,256]{2,1,0:T(8,128)} %fusion.115, f32[32,256,256]{2,1,0:T(8,128)} %get-tuple-element.487, bf16[32,256,1024]{2,1,0:T(8,128)(2,1)} %bitcast.353, bf16[32,256,1024]{2,1,0:T(8,128)(2,1)} %all-gather.17.cloned.1.call-done), kind=kOutput, calls=%fused_computation.80 | convolution fusion | flops 4322230272 | bytes 58720256 | tf_op jit(solution)/shard_map/ecd,efd->ecf/dot_general | solution.py:84
  767.9 19.0 fusion.117
  786.9 30.3 %convolution_add_fusion = f32[32,256,1024]{2,1,0:T(8,128)} fusion(f32[32,256,1024]{2,1,0:T(8,128)} %fusion.117, bf16[32,256,256]{2,1,0:T(8,128)(2,1)} %get-tuple-element.465, bf16[32,1024,256]{2,1,0:T(8,128)(2,1)} %all-gather.15.cloned.1.call-done), kind=kOutput, calls=%fused_computation.73 | convolution fusion | flops 4303355904 | bytes 88080384 | tf_op jit(solution)/shard_map/ecf,edf->ecd/dot_general | solution.py:93
  817.2 32.9 %gather_fusion.2 = f32[4096,1024]{1,0:T(8,128)} fusion(f32[8192,1024]{1,0:T(8,128)} %bitcast.348, s32[4096]{0:T(1024)S(1)} %broadcast_clamp_fusion), kind=kCustom, calls=%fused_computation.3 | custom fusion | bytes 33570816 | tf_op jit(solution)/shard_map/gather | solution.py:247
  850.2 9.5 bitcast_reduce_fusion
  860.1 60.4 %all-reduce.13.cloned.1.call-done = f32[512,1024]{1,0:T(8,128)} async-done(((f32[512,1024]{1,0:T(8,128)}), f32[512,1024]{1,0:T(8,128)}) %all-reduce.13.cloned.1.call-update) | async-done | bytes 2097168 | tf_op jit(solution)/shard_map/psum | solution.py:248
  920.5 2.9 multiply_reduce_fusion.2
  928.5 38.7 %while.37 = (s32[]{:T(128)}, f32[4,1024,64]{1,2,0:T(8,128)}, f32[4,1024,64]{1,2,0:T(8,128)}, f32[4,1024,64]{1,2,0:T(8,128)}, s32[1,512]{1,0:T(1,128)S(1)}, /*ind...) while((s32[]{:T(128)}, f32[4,1024,64]{1,2,0:T(8,128)}, ...), condition=%wide.region_28.29_spmd.clone.clone, body=%wide.region_26.28_spmd.clone.sunk.clone | while | flops 683801600 | bytes 38339768 | solution.py:281
  968.0 2.5 convolution_convert_fusion.3
  972.1 15.1 convolution_convert_fusion
  987.2 24.1 %copy.104 = bf16[32,256,1024]{1,0,2:T(8,128)(2,1)} copy(bf16[32,256,1024]{2,1,0:T(8,128)(2,1)} %convolution_convert_fusion) | data formatting | bytes 33554432
  1011.3 17.8 copy.111
  1029.2 3.2 reshape.564
  1040.3 2.5 convolution_convert_fusion.5
  1042.9 14.7 convolution_convert_fusion.2
  1057.6 14.7 convolution_convert_fusion.1
  1075.0 9.5 fusion.54
  1084.7 2.2 fusion.118
  1091.8 122.0 %reduce-scatter.35.cloned.1.call-done = bf16[128,8192]{1,0:T(8,128)(2,1)} async-done(((bf16[1024,8192]{1,0:T(8,128)(2,1)}), bf16[128,8192]{1,0:T(8,128)(2,1)}) %reduce-scatter.35.cloned.1.call-update) | async-done | bytes 2097168
  1213.7 3.5 copy.112
  1217.3 4.5 copy.105
  1221.8 24.9 %reduce-scatter.21.cloned.1.call-done = bf16[128,512]{1,0:T(8,128)(2,1)} async-done(((bf16[1024,512]{1,0:T(8,128)(2,1)}), bf16[128,512]{1,0:T(8,128)(2,1)}) %reduce-scatter.21.cloned.1.call-update) | async-done | bytes 131088 | tf_op jit(solution)/shard_map/reduce_scatter | solution.py:329
  1246.7 31.3 %reduce-scatter.23.cloned.1.call-done = bf16[128,256]{1,0:T(8,128)(2,1)} async-done(((bf16[1024,256]{1,0:T(8,128)(2,1)}), bf16[128,256]{1,0:T(8,128)(2,1)}) %reduce-scatter.23.cloned.1.call-update) | async-done | bytes 65552 | tf_op jit(solution)/shard_map/reduce_scatter | solution.py:332
  1278.1 31.4 %reduce-scatter.25.cloned.1.call-done = bf16[128,256]{1,0:T(8,128)(2,1)} async-done(((bf16[1024,256]{1,0:T(8,128)(2,1)}), bf16[128,256]{1,0:T(8,128)(2,1)}) %reduce-scatter.25.cloned.1.call-update) | async-done | bytes 65552 | tf_op jit(solution)/shard_map/reduce_scatter | solution.py:335
  1309.4 168.7 %reduce-scatter.27.cloned.1.call-done = bf16[32,128,256]{2,1,0:T(8,128)(2,1)} async-done(((bf16[32,1024,256]{2,1,0:T(8,128)(2,1)}), bf16[32,128,256]{2,1,0:T(8,128)(2,1)}) %reduce-scatter.27.cloned.1.call-update) | async-done | bytes 2097168 | tf_op jit(solution)/shard_map/reduce_scatter | solution.py:349
  1478.1 168.8 %reduce-scatter.29.cloned.1.call-done = bf16[32,128,256]{2,1,0:T(8,128)(2,1)} async-done(((bf16[32,1024,256]{2,1,0:T(8,128)(2,1)}), bf16[32,128,256]{2,1,0:T(8,128)(2,1)}) %reduce-scatter.29.cloned.1.call-update) | async-done | bytes 2097168 | tf_op jit(solution)/shard_map/reduce_scatter | solution.py:352
  1648.2 29.6 %reduce-scatter.33.cloned.1.call-done = bf16[128,32]{1,0:T(8,128)(2,1)} async-done(((bf16[1024,32]{1,0:T(8,128)(2,1)}), bf16[128,32]{1,0:T(8,128)(2,1)}) %reduce-scatter.33.cloned.1.call-update) | async-done | bytes 8208
  1678.6 63.9 %all-reduce.15.cloned.1.call-done = (bf16[512,1024]{1,0:T(8,128)(2,1)}, bf16[512,1024]{1,0:T(8,128)(2,1)}) async-done(((bf16[512,1024]{1,0:T(8,128)(2,1)}, bf16[512,1024]{1,0:T(8,128)(2,1)}), (bf16[512,1024]{1,0:T(8,128)(2,1)}, bf16[512,1024]{1,0:T(8,128)(2,1)})) %all-reduce.15.cloned.1.call-update) | async-done | bytes 2097168 | tf_op jit(solution)/shard_map/psum | solution.py:229
  1744.6 16.4 all-reduce.2
  1761.1 5.3 all-reduce.4
  1768.0 2.5 fusion.79
  1772.5 138.4 %all-reduce.17.cloned.1.call-done = (bf16[128,512]{1,0:T(8,128)(2,1)}, bf16[128,256]{1,0:T(8,128)(2,1)}, bf16[128,256]{1,0:T(8,128)(2,1)}, bf16[512,128]{1,0:T(8...) async-done(((bf16[128,512]{1,0:T(8,128)(2,1)}, bf16[128,256]{1,0:T(8,128)(2,1)}, ...) | async-done | bytes 6684688 | tf_op jit(solution)/shard_map/psum | solution.py:361
  1917.3 4.1 convert_element_type.315
  1921.4 2.5 convert_element_type.317
  1924.0 2.5 convert_element_type.319
  (356 shorter events, 122.4 us)
Async XLA Ops:
  7.2 75.9 %all-gather.9.cloned.1.call-start = ((), (), s32[]{:S(2)}) async-start(), calls=%async_computation.10 | async-start | bytes 1179648 | tf_op jit(solution)/shard_map/all_gather | solution.py:120
  7.9 110.8 %all-gather.11.cloned.1.call-start = ((), (), s32[]{:S(2)}) async-start(), calls=%async_computation.11 | async-start | bytes 1179648 | tf_op jit(solution)/shard_map/all_gather | solution.py:123
  8.7 174.9 %all-reduce.11.cloned.1.call-start = ((), (), s32[]{:S(2)}) async-start(), calls=%async_computation.12 | async-start | bytes 4194304 | tf_op jit(solution)/shard_map/psum | solution.py:197
  26.4 59.0 %copy-start.45 = (f32[8,1,128]{2,1,0:T(1,128)}, f32[8,1,128]{2,1,0:T(1,128)S(1)}, u32[]{:S(2)}) copy-start(f32[8,1,128]{2,1,0:T(1,128)S(1)} %convert_element_type.322) | copy-start | bytes 12292
  27.9 57.4 %copy-start.53 = (f32[512]{0:T(512)}, f32[512]{0:T(512)S(1)}, u32[]{:S(2)}) copy-start(f32[512]{0:T(512)S(1)} %add_rsqrt_fusion.1) | copy-start | bytes 6148
  43.5 13.2 copy-start.11
  45.5 42.0 %copy-start.27 = (f32[512,32]{0,1:T(8,128)}, f32[512,32]{0,1:T(8,128)S(1)}, u32[]{:S(2)}) copy-start(f32[512,32]{0,1:T(8,128)S(1)} %get-tuple-element.485) | copy-start | bytes 196612
  45.5 11.8 copy-start.40
  45.5 27.4 %copy-start.4 = (bf16[1,512,1024]{2,1,0:T(8,128)(2,1)S(1)}, bf16[1,512,1024]{2,1,0:T(8,128)(2,1)}, u32[]{:S(2)}) copy-start(bf16[1,512,1024]{2,1,0:T(8,128)(2,1)} %param.18) | copy-start | bytes 3145732
  85.4 5.4 copy-start.51
  114.1 8.6 copy-start.7
  114.1 8.6 copy-start.9
  114.1 8.6 copy-start.34
  114.1 8.6 copy-start.36
  122.2 214.1 %all-gather.13.cloned.1.call-start = ((), (), s32[]{:S(2)}) async-start(), calls=%async_computation.13 | async-start | bytes 18874368 | tf_op jit(solution)/shard_map/all_gather | solution.py:220
  122.8 12.3 copy-start.57
  122.8 364.3 %all-gather.15.cloned.1.call-start = ((), (), s32[]{:S(2)}) async-start(), calls=%async_computation.14 | async-start | bytes 18874368 | tf_op jit(solution)/shard_map/all_gather | solution.py:221
  123.4 515.3 %all-gather.17.cloned.1.call-start = ((), (), s32[]{:S(2)}) async-start(), calls=%async_computation.15 | async-start | bytes 18874368 | tf_op jit(solution)/shard_map/all_gather | solution.py:222
  124.0 796.5 %all-reduce.13.cloned.1.call-start = ((), (), s32[]{:S(2)}) async-start(), calls=%async_computation.16 | async-start | bytes 4194304 | tf_op jit(solution)/shard_map/psum | solution.py:248
  134.1 10.2 copy-start.12
  144.3 41.3 %copy-start.41 = (f32[8,1,128]{2,1,0:T(1,128)}, f32[8,1,128]{2,1,0:T(1,128)S(1)}, u32[]{:S(2)}) copy-start(f32[8,1,128]{2,1,0:T(1,128)S(1)} %convert_element_type.323) | copy-start | bytes 12292
  145.8 18.7 copy-start.56
  177.4 76.8 %copy-start.30 = (bf16[1024,32]{0,1:T(8,128)(2,1)}, bf16[1024,32]{0,1:T(8,128)(2,1)S(1)}, u32[]{:S(2)}) copy-start(bf16[1024,32]{0,1:T(8,128)(2,1)S(1)} %all_gather.44) | copy-start | bytes 196612
  185.5 68.7 %copy-start.49 = (f32[512]{0:T(512)}, f32[512]{0:T(512)S(1)}, u32[]{:S(2)}) copy-start(f32[512]{0:T(512)S(1)} %add_rsqrt_fusion) | copy-start | bytes 6148
  187.1 67.2 %copy-start.6 = (bf16[512,1024]{1,0:T(8,128)(2,1)}, bf16[512,1024]{1,0:T(8,128)(2,1)S(1)}, u32[]{:S(2)}) copy-start(bf16[512,1024]{1,0:T(8,128)(2,1)S(1)} %multiply_convert_fusion.6) | copy-start | bytes 3145732
  254.7 99.3 %copy-start.43 = (f32[512]{0:T(512)}, f32[512]{0:T(512)S(1)}, u32[]{:S(2)}) copy-start(f32[512]{0:T(512)S(1)} %get-tuple-element.488) | copy-start | bytes 6148
  255.3 98.7 %copy-start.47 = (f32[512]{0:T(512)}, f32[512]{0:T(512)S(1)}, u32[]{:S(2)}) copy-start(f32[512]{0:T(512)S(1)} %fusion.101) | copy-start | bytes 6148
  691.2 23.7 %copy-start.39 = (s32[1,512,8]{1,2,0:T(8,128)S(1)}, s32[1,512,8]{1,2,0:T(8,128)}, u32[]{:S(2)}) copy-start(s32[1,512,8]{1,2,0:T(8,128)} %param.20) | copy-start | bytes 49156
  715.2 30.8 %copy-start.16 = (f32[512,8]{1,0:T(8,128)}, f32[512,8]{1,0:T(8,128)S(1)}, u32[]{:S(2)}) copy-start(f32[512,8]{1,0:T(8,128)S(1)} %copy.86) | copy-start | bytes 49156
  850.2 9.8 copy-start.26
  850.2 9.8 copy-start.44
  850.2 9.8 copy-start.48
  850.2 70.3 %copy-start.1 = (f32[512,1024]{1,0:T(8,128)S(1)}, f32[512,1024]{1,0:T(8,128)}, u32[]{:S(2)}) copy-start(f32[512,1024]{1,0:T(8,128)} %copy-done) | copy-start | bytes 6291460
  850.2 70.3 %copy-start.31 = (bf16[1024,32]{0,1:T(8,128)(2,1)S(1)}, bf16[1024,32]{0,1:T(8,128)(2,1)}, u32[]{:S(2)}) copy-start(bf16[1024,32]{0,1:T(8,128)(2,1)} %copy-done.30) | copy-start | bytes 196612
  850.2 70.3 %copy-start.42 = (f32[8,1,128]{2,1,0:T(1,128)S(1)}, f32[8,1,128]{2,1,0:T(1,128)}, u32[]{:S(2)}) copy-start(f32[8,1,128]{2,1,0:T(1,128)} %copy-done.41) | copy-start | bytes 12292
  850.2 70.3 %copy-start.50 = (f32[512]{0:T(512)S(1)}, f32[512]{0:T(512)}, u32[]{:S(2)}) copy-start(f32[512]{0:T(512)} %copy-done.49) | copy-start | bytes 6148
  859.7 63.8 %copy-start.14 = (bf16[1,512,1024]{2,1,0:T(8,128)(2,1)S(1)}, bf16[1,512,1024]{2,1,0:T(8,128)(2,1)}, u32[]{:S(2)}) copy-start(bf16[1,512,1024]{2,1,0:T(8,128)(2,1)} %param.31) | copy-start | bytes 3145732
  859.7 177.2 %reduce-scatter.17.cloned.1.call-start = ((), (), s32[]{:S(2)}) async-start(), calls=%async_computation.17 | async-start | bytes 1572864 | tf_op jit(solution)/shard_map/reduce_scatter | solution.py:295
  925.4 3.1 copy-start.35
  925.4 3.1 copy-start.37
  925.4 3.1 copy-start.52
  967.2 73.1 %reduce-scatter.19.cloned.1.call-start = ((), (), s32[]{:S(2)}) async-start(), calls=%async_computation.18 | async-start | bytes 1572864 | tf_op jit(solution)/shard_map/reduce_scatter | solution.py:296
  968.0 122.2 %reduce-scatter.31.cloned.1.call-start = ((), (), s32[]{:S(2)}) async-start(), calls=%async_computation.24 | async-start | bytes 1179648
  971.8 241.9 %reduce-scatter.35.cloned.1.call-start = ((), (), s32[]{:S(2)}) async-start(), calls=%async_computation.26 | async-start | bytes 18874368
  1029.1 4.7 copy-start.28
  1029.1 4.7 copy-start.32
  1029.2 5.7 copy-start.5
  1029.2 5.7 copy-start.46
  1029.2 5.7 copy-start.54
  1029.2 217.5 %reduce-scatter.21.cloned.1.call-start = ((), (), s32[]{:S(2)}) async-start(), calls=%async_computation.19 | async-start | bytes 1179648 | tf_op jit(solution)/shard_map/reduce_scatter | solution.py:329
  1036.8 241.3 %reduce-scatter.23.cloned.1.call-start = ((), (), s32[]{:S(2)}) async-start(), calls=%async_computation.20 | async-start | bytes 589824 | tf_op jit(solution)/shard_map/reduce_scatter | solution.py:332
  1040.2 269.2 %reduce-scatter.25.cloned.1.call-start = ((), (), s32[]{:S(2)}) async-start(), calls=%async_computation.21 | async-start | bytes 589824 | tf_op jit(solution)/shard_map/reduce_scatter | solution.py:335
  1042.8 435.3 %reduce-scatter.27.cloned.1.call-start = ((), (), s32[]{:S(2)}) async-start(), calls=%async_computation.22 | async-start | bytes 18874368 | tf_op jit(solution)/shard_map/reduce_scatter | solution.py:349
  1057.6 589.4 %reduce-scatter.29.cloned.1.call-start = ((), (), s32[]{:S(2)}) async-start(), calls=%async_computation.23 | async-start | bytes 18874368 | tf_op jit(solution)/shard_map/reduce_scatter | solution.py:352
  1072.3 605.5 %reduce-scatter.33.cloned.1.call-start = ((), (), s32[]{:S(2)}) async-start(), calls=%async_computation.25 | async-start | bytes 294912
  1084.6 657.9 %all-reduce.15.cloned.1.call-start = ((), (), s32[]{:S(2)}) async-start(), calls=%async_computation.27 | async-start | bytes 4194304 | tf_op jit(solution)/shard_map/psum | solution.py:229
  1084.6 3.9 copy-start.21
  1084.6 3.9 copy-start.33
  1090.0 820.8 %all-reduce.17.cloned.1.call-start = ((), (), s32[]{:S(2)}) async-start(), calls=%async_computation.28 | async-start | bytes 13369344 | tf_op jit(solution)/shard_map/psum | solution.py:361
  1221.8 425.2 %copy-start.58 = (u32[32]{0:T(128)S(1)}, u32[32]{0:T(128)}, u32[]{:S(2)}) copy-start(u32[32]{0:T(128)} %constant.191) | copy-start | bytes 388
  1646.9 97.6 %copy-start.55 = (bf16[1024]{0:T(1024)(128)(2,1)S(1)}, bf16[1024]{0:T(1024)(128)(2,1)}, u32[]{:S(2)}) copy-start(bf16[1024]{0:T(1024)(128)(2,1)} %get-tuple-element.397) | copy-start | bytes 6148
  1766.3 4.2 copy-start.3
  1766.4 4.2 copy-start.15
  1910.9 10.5 copy-start.19
  (26 other events, 49.7 us)
Sparse Core Ops, SparseCore 0:
  9.6 25.3 all-gather.8
  36.6 23.7 all-gather.10
  122.3 61.2 all-reduce.10
  185.1 151.1 all-gather.12
  337.8 149.2 all-gather.14
  488.7 149.9 all-gather.16
  859.8 60.6 all-reduce.12
  967.3 20.3 reduce-scatter.16
  990.0 20.3 reduce-scatter.18
  1012.5 32.4 reduce-scatter.30
  1047.3 166.3 reduce-scatter.34
  1215.9 30.7 reduce-scatter.20
  1249.0 29.0 reduce-scatter.22
  1280.3 29.1 reduce-scatter.24
  1311.6 166.4 reduce-scatter.26
  1480.3 166.5 reduce-scatter.28
  1649.0 28.7 reduce-scatter.32
  1681.3 61.2 all-reduce.14
  1746.8 164.0 all-reduce.16
where the time goes:
time: 1940 us; the launch traced here: 1930 us
  waiting for transfers between devices  1190 us (61%)
  matrix products  246 us (13%)
  local copies, waits for them, and re-layouts  244 us (13%)
  blocking collectives  118 us (6%)
  other arithmetic  116 us (6%)
    reduce_scatter x1, waiting for transfers between devices, body(): lax.psum_scatter(grad_up.astype(jnp.bfloat16), 'fsdp', scatter_dimension=...  169 us
    reduce_scatter x1, waiting for transfers between devices, body(): lax.psum_scatter(grad_gate.astype(jnp.bfloat16), 'fsdp', scatter_dimensio...  169 us
    unnamed x22, waiting for transfers between devices  155 us
    psum x1, waiting for transfers between devices, body(): lax.psum(dense[1].astype(jnp.bfloat16), 'ctx').astype(jnp.float32)  138 us
    all_gather x1, waiting for transfers between devices, body(): lax.all_gather(w_up, 'fsdp', axis=1, tiled=True)  133 us
    all_gather x1, waiting for transfers between devices, body(): lax.all_gather(w_down, 'fsdp', axis=2, tiled=True)  129 us
    all_gather x1, waiting for transfers between devices, body(): lax.all_gather(w_gate, 'fsdp', axis=1, tiled=True)  80.9 us
    scatter x1, local copies, waits for them, and re-layouts, body(): buffer = jnp.zeros((E * capacity, model_width), jnp.bfloat16).at[slot_ind...  67.1 us
  transfers between devices with their start and end apart: 19, of which 14 were waited for; matrix products, arithmetic and copies ran while one was open for 17% of the time, Pallas kernels for 0%

commit v1 on v0

v1 whole, which is shorter than its diff:
```python
import jax
import jax.numpy as jnp
from jax import lax
from jax.sharding import PartitionSpec as P

HD = 64
E = 32
TOPK = 8


epsilon = 1e-05
rope_base = 10000.0
masked_fill = -1e30


def matmul(left, right):
    return jnp.dot(left, right, preferred_element_type=jnp.float32)


def contract_rows(left, right):
    return lax.dot_general(
        left, right, (((0,), (0,)), ((), ())), preferred_element_type=jnp.float32
    )


def contract_cols(left, right):
    return lax.dot_general(
        left, right, (((1,), (1,)), ((), ())), preferred_element_type=jnp.float32
    )


def rms_factor(values):
    return lax.rsqrt(jnp.mean(values * values, axis=-1, keepdims=True) + epsilon)


def doc_positions(segments):
    index = lax.broadcasted_iota(jnp.int32, segments.shape, 1)
    earlier = jnp.concatenate([segments[:, :1], segments[:, :-1]], axis=1)
    starts = jnp.where((segments != earlier) | (index == 0), index, 0)
    return index - lax.cummax(starts, axis=1)


def rotary_tables(positions, head_size):
    half_size = head_size // 2
    exponent = jnp.arange(half_size, dtype=jnp.float32) * (-2.0 / head_size)
    angles = positions.astype(jnp.float32)[..., None] * jnp.power(rope_base, exponent)
    return (jnp.cos(angles), jnp.sin(angles))


def rotate(values, cosine, sine_tab):
    half_size = values.shape[-1] // 2
    first_half = values[..., :half_size]
    second_half = values[..., half_size:]
    cos_wide = cosine[..., None, :]
    sin_wide = sine_tab[..., None, :]
    return jnp.concatenate(
        [
            first_half * cos_wide - second_half * sin_wide,
            second_half * cos_wide + first_half * sin_wide,
        ],
        axis=-1,
    )


def norm_backward(grad_normed, normed, factor, gain):
    scaled = grad_normed * gain
    return factor * (scaled - normed * jnp.mean(scaled * normed, axis=-1, keepdims=True))


def column_pack(shards, groups):
    experts, depth, units = shards.shape
    local = experts // groups
    return (
        shards.reshape(groups, local, depth, units)
        .transpose(0, 2, 1, 3)
        .reshape(groups, depth, local * units)
    )


def column_unpack(packed, units):
    groups, depth, columns = packed.shape
    local = columns // units
    return (
        packed.reshape(groups, depth, local, units)
        .transpose(0, 2, 1, 3)
        .reshape(groups * local, depth, units)
    )


def gather_experts(shards, groups, ctx_count):
    packed = column_pack(shards, groups)
    part = packed.shape[2] // ctx_count
    mine = lax.dynamic_slice_in_dim(packed, lax.axis_index("ctx") * part, part, 2)
    moved = lax.all_to_all(mine, "fsdp", split_axis=0, concat_axis=0, tiled=True)
    return lax.all_gather(moved.reshape(-1, part), "ctx", axis=1, tiled=True)


def return_experts(grad, groups, units):
    summed = lax.psum_scatter(
        grad.astype(jnp.bfloat16), "ctx", scatter_dimension=1, tiled=True
    )
    depth = summed.shape[0] // groups
    moved = lax.all_to_all(
        summed.reshape(groups, depth, -1), "fsdp", split_axis=0, concat_axis=0, tiled=True
    )
    return column_unpack(lax.all_gather(moved, "ctx", axis=2, tiled=True), units)


def router_probs(normed, router_w):
    logits = matmul(normed, router_w)
    exp_logits = jnp.exp(logits - jnp.max(logits, axis=-1, keepdims=True))
    return exp_logits / jnp.sum(exp_logits, axis=-1, keepdims=True)


def body(
    hidden_in,
    segment_ids,
    expert_ids,
    norm1_gain,
    w_query,
    w_key,
    w_value,
    w_output,
    norm2_gain,
    w_router,
    w_gate,
    w_up,
    w_down,
    cotangent,
):
    row_count, ctx_tok, model_width = hidden_in.shape
    tok_count = row_count * ctx_tok
    seq_len = segment_ids.shape[1]
    first_pos = lax.axis_index("ctx") * ctx_tok
    score_scale = HD ** (-0.5)
    groups = lax.axis_size("fsdp")
    ctx_count = lax.axis_size("ctx")
    hidden_units = w_gate.shape[2]
    q_cols, k_cols, o_cols = w_query.shape[1], w_key.shape[1], w_output.shape[0]
    small_at = q_cols + 2 * k_cols + o_cols
    shard_rows = w_query.shape[0]
    packed_w = lax.all_gather(
        jnp.concatenate(
            [
                w_query,
                w_key,
                w_value,
                w_output.T,
                w_router,
                norm1_gain[:, None],
                norm2_gain[:, None],
                jnp.zeros((shard_rows, 128 - E - 2), jnp.bfloat16),
            ],
            axis=1,
        ),
        "fsdp",
        axis=0,
        tiled=True,
    )
    query_w = packed_w[:, :q_cols]
    key_w = packed_w[:, q_cols : q_cols + k_cols]
    value_w = packed_w[:, q_cols + k_cols : q_cols + 2 * k_cols]
    out_wt = packed_w[:, q_cols + 2 * k_cols : small_at]
    router_w = packed_w[:, small_at : small_at + E]
    gain_one = packed_w[:, small_at + E]
    gain_two = packed_w[:, small_at + E + 1]
    token_ids = expert_ids.reshape(tok_count, TOPK)
    route_mask = jnp.sum(
        (token_ids[:, :, None] == jnp.arange(E, dtype=jnp.int32)).astype(jnp.float32), axis=1
    )
    mask_all = lax.all_gather(route_mask.astype(jnp.bfloat16), "fsdp", axis=0, tiled=True)
    grad_all = lax.all_gather(
        cotangent.reshape(tok_count, model_width), "fsdp", axis=0, tiled=True
    )
    down_wt = gather_experts(w_down.transpose(0, 2, 1), groups, ctx_count)
    gate_w = gather_experts(w_gate, groups, ctx_count)
    up_w = gather_experts(w_up, groups, ctx_count)
    inputs = hidden_in.reshape(tok_count, model_width).astype(jnp.float32)
    factor_one = rms_factor(inputs)
    normed_one = inputs * factor_one
    first_in = (normed_one * gain_one.astype(jnp.float32)).astype(jnp.bfloat16)
    query_lin = matmul(first_in, query_w)
    key_lin = matmul(first_in, key_w)
    values = matmul(first_in, value_w).astype(jnp.bfloat16)
    heads_q = query_lin.shape[1] // HD
    heads_k = key_lin.shape[1] // HD
    group_size = heads_q // heads_k
    positions = doc_positions(segment_ids)
    local_pos = lax.dynamic_slice_in_dim(positions, first_pos, ctx_tok, 1).reshape(tok_count)
    cosine, sine_tab = rotary_tables(local_pos, HD)
    queries = rotate(query_lin.reshape(tok_count, heads_q, HD), cosine, sine_tab).astype(
        jnp.bfloat16
    )
    keys_rot = rotate(key_lin.reshape(tok_count, heads_k, HD), cosine, sine_tab).astype(
        jnp.bfloat16
    )
    kv_all = lax.all_gather(
        jnp.concatenate([keys_rot.reshape(tok_count, heads_k * HD), values], axis=1).reshape(
            row_count, ctx_tok, 2 * heads_k * HD
        ),
        "ctx",
        axis=1,
        tiled=True,
    )
    keys_all, values_all = kv_all[..., : heads_k * HD], kv_all[..., heads_k * HD :]
    pair_count = row_count * heads_k
    query_pairs = (
        queries.reshape(row_count, ctx_tok, heads_k, group_size, HD)
        .transpose(0, 2, 3, 1, 4)
        .reshape(pair_count, group_size * ctx_tok, HD)
    )
    key_pairs = (
        keys_all.reshape(row_count, seq_len, heads_k, HD)
        .transpose(0, 2, 1, 3)
        .reshape(pair_count, seq_len, HD)
    )
    value_pairs = (
        values_all.reshape(row_count, seq_len, heads_k, HD)
        .transpose(0, 2, 1, 3)
        .reshape(pair_count, seq_len, HD)
    )
    row_of = jnp.arange(pair_count, dtype=jnp.int32) // heads_k
    key_index = jnp.arange(seq_len, dtype=jnp.int32)
    query_index = jnp.tile(first_pos + jnp.arange(ctx_tok, dtype=jnp.int32), group_size)

    def pair_scores(query_block, key_block, row_pick):
        seg_row = lax.dynamic_index_in_dim(segment_ids, row_pick, 0, keepdims=False)
        seg_query = jnp.tile(lax.dynamic_slice_in_dim(seg_row, first_pos, ctx_tok), group_size)
        allowed = (key_index[None, :] <= query_index[:, None]) & (
            seg_query[:, None] == seg_row[None, :]
        )
        raw_scores = contract_cols(query_block, key_block) * score_scale
        return jnp.where(allowed, raw_scores, masked_fill)

    def forward_pair(parts_in):
        query_block, key_block, value_block, row_pick = parts_in
        scores = pair_scores(query_block, key_block, row_pick)
        row_max = jnp.max(scores, axis=-1, keepdims=True)
        exp_vals = jnp.exp(scores - row_max)
        totals = jnp.sum(exp_vals, axis=-1, keepdims=True)
        weights_p = (exp_vals / totals).astype(jnp.bfloat16)
        return (matmul(weights_p, value_block), (row_max + jnp.log(totals))[:, 0])

    mixture, log_totals = lax.map(forward_pair, (query_pairs, key_pairs, value_pairs, row_of))
    att_out = (
        mixture.reshape(row_count, heads_k, group_size, ctx_tok, HD)
        .transpose(0, 3, 1, 2, 4)
        .reshape(tok_count, heads_q * HD)
        .astype(jnp.bfloat16)
    )
    resid = inputs + lax.psum(
        contract_cols(att_out, out_wt).astype(jnp.bfloat16), "tp"
    ).astype(jnp.float32)
    factor_two = rms_factor(resid)
    normed_two = resid * factor_two
    second_in = (normed_two * gain_two.astype(jnp.float32)).astype(jnp.bfloat16)
    router = router_probs(second_in, router_w)
    normed_all = lax.all_gather(second_in, "fsdp", axis=0, tiled=True)
    columns = gate_w.shape[1]
    column_expert = lax.axis_index("fsdp") * (columns // hidden_units) + (
        jnp.arange(columns, dtype=jnp.int32) // hidden_units
    )
    owner = (jnp.arange(E, dtype=jnp.int32)[:, None] == column_expert[None, :]).astype(
        jnp.float32
    )
    grad_mid = matmul(grad_all, down_wt)
    gates_all = router_probs(normed_all, router_w) * mask_all.astype(jnp.float32)
    gate_cols = jnp.dot(
        gates_all, owner, precision=lax.Precision.HIGHEST, preferred_element_type=jnp.float32
    )
    gate_pre = matmul(normed_all, gate_w)
    up_pre = matmul(normed_all, up_w)
    sigmoid_g = jax.nn.sigmoid(gate_pre)
    activated = gate_pre * sigmoid_g
    hidden = activated * up_pre
    weighted = (hidden * gate_cols).astype(jnp.bfloat16)
    grad_hidden = grad_mid * gate_cols
    grad_gate_pre = (
        grad_hidden * up_pre * sigmoid_g * (1.0 + gate_pre * (1.0 - sigmoid_g))
    ).astype(jnp.bfloat16)
    grad_up_pre = (grad_hidden * activated).astype(jnp.bfloat16)
    gate_grad_all = contract_cols(
        (hidden * grad_mid).astype(jnp.bfloat16), owner.astype(jnp.bfloat16)
    )
    grad_route = (
        lax.psum_scatter(gate_grad_all, "fsdp", scatter_dimension=0, tiled=True) * route_mask
    )
    grad_rows = contract_cols(grad_gate_pre, gate_w) + contract_cols(grad_up_pre, up_w)
    grad_in_part = lax.psum_scatter(
        grad_rows.astype(jnp.bfloat16), "fsdp", scatter_dimension=0, tiled=True
    )
    moe_rows = contract_cols(weighted, down_wt).astype(jnp.bfloat16)
    moe_rows, _ = lax.optimization_barrier((moe_rows, grad_in_part))
    moe_part = lax.psum_scatter(moe_rows, "fsdp", scatter_dimension=0, tiled=True)
    gate_part = return_experts(contract_rows(normed_all, grad_gate_pre), groups, hidden_units)
    up_part = return_experts(contract_rows(normed_all, grad_up_pre), groups, hidden_units)
    down_part = return_experts(
        contract_rows(grad_all, weighted), groups, hidden_units
    ).transpose(0, 2, 1)
    grad_out = cotangent.reshape(tok_count, model_width).astype(jnp.float32)
    grad_logits = (
        router * (grad_route - jnp.sum(router * grad_route, axis=-1, keepdims=True))
    ).astype(jnp.bfloat16)
    grad_router = contract_rows(second_in, grad_logits)
    grad_second = lax.psum(
        (grad_in_part.astype(jnp.float32) + contract_cols(grad_logits, router_w)).astype(
            jnp.bfloat16
        ),
        "tp",
    ).astype(jnp.float32)
    moe_part, _ = lax.optimization_barrier((moe_part, grad_second))
    moe_total = lax.psum(moe_part, "tp").astype(jnp.float32)
    block_out = (resid + moe_total).astype(jnp.bfloat16).reshape(row_count, ctx_tok, model_width)
    grad_gain_two = jnp.sum(grad_second * normed_two, axis=0)
    grad_resid = grad_out + norm_backward(
        grad_second, normed_two, factor_two, gain_two.astype(jnp.float32)
    )
    grad_att = grad_resid.astype(jnp.bfloat16)
    grad_out_wt = contract_rows(grad_att, att_out)
    grad_att_out = matmul(grad_att, out_wt).astype(jnp.bfloat16)
    grad_out_pairs = (
        grad_att_out.reshape(row_count, ctx_tok, heads_k, group_size, HD)
        .transpose(0, 2, 3, 1, 4)
        .reshape(pair_count, group_size * ctx_tok, HD)
    )

    def backward_pair(parts_in):
        query_block, key_block, value_block, grad_block, log_row, row_pick = parts_in
        scores = pair_scores(query_block, key_block, row_pick)
        weights_p = jnp.exp(scores - log_row[:, None])
        grad_p = contract_cols(grad_block, value_block)
        grad_v = contract_rows(weights_p.astype(jnp.bfloat16), grad_block)
        grad_s = (
            weights_p * (grad_p - jnp.sum(weights_p * grad_p, axis=-1, keepdims=True))
        ).astype(jnp.bfloat16)
        grad_q = matmul(grad_s, key_block) * score_scale
        grad_k = contract_rows(grad_s, query_block) * score_scale
        return (grad_q, grad_k, grad_v)

    grad_q_pairs, grad_k_pairs, grad_v_pairs = lax.map(
        backward_pair, (query_pairs, key_pairs, value_pairs, grad_out_pairs, log_totals, row_of)
    )
    grad_k_rows = (
        grad_k_pairs.reshape(row_count, heads_k, seq_len, HD)
        .transpose(0, 2, 1, 3)
        .reshape(row_count, seq_len, heads_k * HD)
    )
    grad_v_rows = (
        grad_v_pairs.reshape(row_count, heads_k, seq_len, HD)
        .transpose(0, 2, 1, 3)
        .reshape(row_count, seq_len, heads_k * HD)
    )
    own_kv = lax.psum_scatter(
        jnp.concatenate([grad_k_rows, grad_v_rows], axis=2).astype(jnp.bfloat16),
        "ctx",
        scatter_dimension=1,
        tiled=True,
    ).astype(jnp.float32)
    own_k, own_v = own_kv[..., : heads_k * HD], own_kv[..., heads_k * HD :]
    grad_q_rot = (
        grad_q_pairs.reshape(row_count, heads_k, group_size, ctx_tok, HD)
        .transpose(0, 3, 1, 2, 4)
        .reshape(tok_count, heads_q, HD)
    )
    grad_query_lin = (
        rotate(grad_q_rot, cosine, -sine_tab).reshape(tok_count, heads_q * HD).astype(jnp.bfloat16)
    )
    grad_key_lin = (
        rotate(own_k.reshape(tok_count, heads_k, HD), cosine, -sine_tab)
        .reshape(tok_count, heads_k * HD)
        .astype(jnp.bfloat16)
    )
    grad_value_lin = own_v.reshape(tok_count, heads_k * HD).astype(jnp.bfloat16)
    grad_qkv = contract_rows(
        first_in, jnp.concatenate([grad_query_lin, grad_key_lin, grad_value_lin], axis=1)
    )
    grad_first_part = (
        contract_cols(grad_query_lin, query_w)
        + contract_cols(grad_key_lin, key_w)
        + contract_cols(grad_value_lin, value_w)
    )
    grad_first_part, _ = lax.optimization_barrier((grad_first_part, moe_total))
    grad_first = lax.psum(grad_first_part.astype(jnp.bfloat16), "tp").astype(jnp.float32)
    grad_input = grad_resid + norm_backward(
        grad_first, normed_one, factor_one, gain_one.astype(jnp.float32)
    )
    grad_gain_one = jnp.sum(grad_first_part * normed_one, axis=0)
    counted = (lax.axis_index("tp") == 0).astype(jnp.float32)
    dense = lax.psum_scatter(
        jnp.concatenate(
            [
                grad_qkv.astype(jnp.bfloat16),
                grad_out_wt.astype(jnp.bfloat16),
                grad_router.astype(jnp.bfloat16),
                grad_gain_one.astype(jnp.bfloat16)[:, None],
                (grad_gain_two * counted).astype(jnp.bfloat16)[:, None],
                jnp.zeros((model_width, 128 - E - 2), jnp.bfloat16),
            ],
            axis=1,
        ),
        "fsdp",
        scatter_dimension=0,
        tiled=True,
    )
    large = lax.psum(dense[:, :small_at], "ctx").astype(jnp.float32)
    small = lax.psum(dense[:, small_at:], ("ctx", "tp")).astype(jnp.float32)
    return (
        block_out,
        grad_input.reshape(row_count, ctx_tok, model_width),
        small[:, E],
        large[:, :q_cols],
        large[:, q_cols : q_cols + k_cols],
        large[:, q_cols + k_cols : q_cols + 2 * k_cols],
        large[:, q_cols + 2 * k_cols :].T,
        small[:, E + 1],
        small[:, :E],
        gate_part.astype(jnp.float32),
        up_part.astype(jnp.float32),
        down_part.astype(jnp.float32),
    )


def solution(mesh):
    placed = (
        P("fsdp", "ctx", None),
        P("fsdp", None),
        P("fsdp", "ctx", None),
        P("fsdp"),
        P("fsdp", "tp"),
        P("fsdp", "tp"),
        P("fsdp", "tp"),
        P("tp", "fsdp"),
        P("fsdp"),
        P("fsdp", None),
        P(None, "fsdp", "tp"),
        P(None, "fsdp", "tp"),
        P(None, "tp", "fsdp"),
        P("fsdp", "ctx", None),
    )
    return jax.shard_map(
        body,
        mesh=mesh,
        in_specs=placed,
        out_specs=(
            P("fsdp", "ctx", None),
            P("fsdp", "ctx", None),
            P("fsdp"),
            P("fsdp", "tp"),
            P("fsdp", "tp"),
            P("fsdp", "tp"),
            P("tp", "fsdp"),
            P("fsdp"),
            P("fsdp", None),
            P(None, "fsdp", "tp"),
            P(None, "fsdp", "tp"),
            P(None, "tp", "fsdp"),
        ),
        check_vma=False,
    )
```

time: 1940 us -> 1240 us (0.64)
  waiting for transfers between devices: 1190 us -> 634 us
  local copies, waits for them, and re-layouts: 244 us -> 109 us
  other arithmetic: 116 us -> 40 us
  blocking collectives: 118 us -> 155 us
  matrix products: 246 us -> 267 us
    reduce_scatter x7, waiting for transfers between devices: 425 us -> 189 us  [the longest x1 87.8 us: body(): lax.psum_scatter(grad_rows.astype(jnp.bfloat16), 'fsdp', scatter_dimensio...]
    psum x4, waiting for transfers between devices: 267 us -> 70.2 us  [the longest x1 38.5 us: body(): lax.psum((grad_in_part.astype(jnp.float32) + contract_cols(grad_logits, r...]
    dot_general x9 -> x1, matrix products: 175 us -> 28.8 us  [body(): jnp.dot(gates_all, owner, precision=lax.Precision.HIGHEST, preferred_elem...]
    all_to_all x0 -> x4, blocking collectives: none -> 125 us  [the longest x3 93.9 us: return_experts(): lax.all_to_all(summed.reshape(groups, depth, -1), 'fsdp', split_axis=0, c...]
    unnamed x22 -> x23, waiting for transfers between devices: 155 us -> 41.3 us
    gather x3 -> x0, local copies, waits for them, and re-layouts: 84.5 us -> none  [the longest x1 33 us: body(): routed = flat_out[slot_index].reshape(tok_count, TOPK, model_width)]
    all_gather x7 -> x1, blocking collectives: 84.6 us -> 14.2 us  [body(): lax.all_gather(route_mask.astype(jnp.bfloat16), 'fsdp', axis=0, tiled=True)]
    scatter x1 -> x0, local copies, waits for them, and re-layouts: 67.1 us -> none  [body(): buffer = jnp.zeros((E * capacity, model_width), jnp.bfloat16).at[slot_ind...]
  transfers between devices with their start and end apart: 19 -> 24, of which waited for: 14 -> 21; matrix products, arithmetic and copies ran while one was open for 17% -> 20% of each run, Pallas kernels for 0% -> 0%
where the time goes in v1:
time: 1240 us; the launch traced here: 1230 us
  waiting for transfers between devices  634 us (51%)
  matrix products  267 us (22%)
  blocking collectives  155 us (12%)
  local copies, waits for them, and re-layouts  109 us (9%)
  other arithmetic  40 us (3%)
  between operations  15.7 us (1%)
    dot_general x21, matrix products, contract_cols(): lax.dot_general(left, right, (((1,), (1,)), ((), ())), preferred_element_...  98.2 us
    all_to_all x3, blocking collectives, return_experts(): lax.all_to_all(summed.reshape(groups, depth, -1), 'fsdp', split_axis=0, c...  93.9 us
    reduce_scatter x1, waiting for transfers between devices, body(): lax.psum_scatter(grad_rows.astype(jnp.bfloat16), 'fsdp', scatter_dimensio...  87.8 us
    all_gather x1, waiting for transfers between devices, body(): normed_all = lax.all_gather(second_in, 'fsdp', axis=0, tiled=True)  84.4 us
    dot_general x17, matrix products, matmul(): return jnp.dot(left, right, preferred_element_type=jnp.float32)  80.7 us
    all_gather x1, waiting for transfers between devices, body(): lax.all_gather(cotangent.reshape(tok_count, model_width), 'fsdp', axis=0,...  78 us
    all_gather x3, waiting for transfers between devices, return_experts(): lax.all_gather(moved, 'ctx', axis=2, tiled=True)  64.2 us
    dot_general x14, matrix products, contract_rows(): lax.dot_general(left, right, (((0,), (0,)), ((), ())), preferred_element_...  59.1 us
  transfers between devices with their start and end apart: 24, of which 21 were waited for; matrix products, arithmetic and copies ran while one was open for 20% of the time, Pallas kernels for 0%

profile of v1, /device:TPU:0, one launch (start us, length us, event | category | flops | bytes accessed | tf_op | source)
XLA Modules:
  0.0 1231.3 jit_solution(7133931061396212540)
XLA Ops:
  10.2 7.5 concatenate.73
  21.0 3.1 copy.118
  24.1 2.7 reshape.524
  28.2 33.7 %all-gather.13.cloned.1.call-done = bf16[1024,1664]{0,1:T(8,128)(2,1)} async-done(((bf16[128,1664]{0,1:T(8,128)(2,1)}), bf16[1024,1664]{0,1:T(8,128)(2,1)}) %all-gather.13.cloned.1.call-update) | async-done | bytes 3407888 | tf_op jit(solution)/shard_map/all_gather | solution.py:142
  68.4 4.2 all-to-all-start.2
  76.0 10.8 all-gather.29.cloned.1.call-done
  95.3 36.8 %while.36 = (s32[]{:T(128)}, bf16[4,1024,64]{1,2,0:T(8,128)(2,1)}, f32[4,1024]{1,0:T(4,128)}, s32[1,512]{1,0:T(1,128)S(1)}, s32[1,1024]{1,0:T(1,128)S(1)}, /*ind...) while((s32[]{:T(128)}, bf16[4,1024,64]{1,2,0:T(8,128)(2,1)}, ...), condition=%wide.region_6.7_spmd.clone.clone, body=%wide.region_3.6_spmd.clone.sunk.clone | while | flops 279968768 | bytes 30492796 | solution.py:244
  100.8 3.7 fusion.206
  110.0 3.7 fusion.206
  119.2 3.7 fusion.206
  128.4 3.7 fusion.206
  132.1 2.6 convert_element_type.284
  136.6 2.9 convolution_convert_fusion.5
  140.8 3.2 copy.116
  144.1 31.0 %all_to_all.30 = bf16[8,128,512]{1,2,0:T(8,128)(2,1)S(1)} all-to-all(bf16[8,128,512]{1,2,0:T(8,128)(2,1)S(1)} %constant_dynamic-slice_fusion.2), channel_id=1, replica_groups=mesh['fsdp'=8,'ctx'=2,'tp'=2] {'fsdp'}, dimensions={0} | all-to-all | bytes 2097152 | tf_op jit(solution)/shard_map/all_to_all | solution.py:94
  176.5 3.3 all-reduce.6.cloned.1.call-done
  183.0 3.2 copy.114
  187.2 4.6 all-to-all-start
  191.9 26.5 %all-to-all-done = bf16[8,128,512]{1,2,0:T(8,128)(2,1)S(1)} async-done(((bf16[8,128,512]{1,2,0:T(8,128)(2,1)}), bf16[8,128,512]{1,2,0:T(8,128)(2,1)S(1)}, u32[]{:S(2)}, u32[]{:S(2)}) %all-to-all-start) | async-done | bytes 1048608 | tf_op jit(solution)/shard_map/all_to_all | solution.py:94
  220.0 78.0 %all-gather.31.cloned.1.call-done = bf16[1,4096,1024]{2,1,0:T(8,128)(2,1)} async-done(((bf16[1,512,1024]{2,1,0:T(8,128)(2,1)}), bf16[1,4096,1024]{2,1,0:T(8,128)(2,1)}) %all-gather.31.cloned.1.call-update) | async-done | bytes 8388624 | tf_op jit(solution)/shard_map/all_gather | solution.py:172
  298.0 16.1 %fusion.60 = f32[1024,4096]{0,1:T(8,128)} fusion(bf16[1024,1024]{1,0:T(8,128)(2,1)} %all-gather.21.cloned.1.call-done, bf16[1,4096,1024]{2,1,0:T(8,128)(2,1)} %all-gather.31.cloned.1.call-done), kind=kOutput, calls=%fused_computation.74 | convolution fusion | flops 8589934592 | bytes 27262976 | tf_op jit(solution)/shard_map/dot_general | solution.py:17
  314.1 17.7 %all-gather.19.cloned.1.call-done = bf16[1024,1024]{1,0:T(8,128)(2,1)} async-done(((bf16[1024,512]{1,0:T(8,128)(2,1)}), bf16[1024,1024]{1,0:T(8,128)(2,1)}) %all-gather.19.cloned.1.call-update) | async-done | bytes 2097168 | tf_op jit(solution)/shard_map/all_gather | solution.py:95
  331.8 84.4 %all-gather.15.cloned.1.call-done = bf16[4096,1024]{1,0:T(8,128)(2,1)} async-done(((bf16[512,1024]{1,0:T(8,128)(2,1)}), bf16[4096,1024]{1,0:T(8,128)(2,1)}) %all-gather.15.cloned.1.call-update) | async-done | bytes 8388624 | tf_op jit(solution)/shard_map/all_gather | solution.py:258
  416.1 16.1 %fusion.140 = f32[4096,1024]{1,0:T(8,128)} fusion(bf16[4096,1024]{1,0:T(8,128)(2,1)} %all-gather.15.cloned.1.call-done, bf16[1024,1024]{1,0:T(8,128)(2,1)} %all-gather.19.cloned.1.call-done), kind=kOutput, calls=%fused_computation.224 | convolution fusion | flops 8589934592 | bytes 27262976 | tf_op jit(solution)/shard_map/dot_general | solution.py:17
  432.2 17.8 %all-gather.17.cloned.1.call-done = bf16[1024,1024]{1,0:T(8,128)(2,1)} async-done(((bf16[1024,512]{1,0:T(8,128)(2,1)}), bf16[1024,1024]{1,0:T(8,128)(2,1)}) %all-gather.17.cloned.1.call-update) | async-done | bytes 2097168 | tf_op jit(solution)/shard_map/all_gather | solution.py:95
  450.0 16.3 %fusion.139 = f32[4096,1024]{1,0:T(8,128)} fusion(bf16[4096,1024]{1,0:T(8,128)(2,1)} %all-gather.15.cloned.1.call-done, bf16[1024,1024]{1,0:T(8,128)(2,1)} %all-gather.17.cloned.1.call-done), kind=kOutput, calls=%fused_computation.223 | convolution fusion | flops 8589934592 | bytes 27262976 | tf_op jit(solution)/shard_map/dot_general | solution.py:17
  466.3 18.7 %fusion.56 = f32[4096,32]{0,1:T(8,128)} fusion(f32[1024,4096]{0,1:T(8,128)} %fusion.60, f32[4096,1024]{1,0:T(8,128)} %fusion.140, s32[1024]{0:T(1024)S(1)} %fusion.119, f32[4096,1024]{1,0:T(8,128)} %fusion.139), kind=kOutput, calls=%fused_computation.71 | convolution fusion | flops 297893888 | bytes 50860032 | tf_op jit(solution)/shard_map/dot_general | solution.py:27
  486.5 6.0 fusion.138
  492.6 23.6 %reduce-scatter.15.cloned.1.call-done = f32[512,32]{0,1:T(8,128)} async-done(((f32[4096,32]{0,1:T(8,128)}), f32[512,32]{0,1:T(8,128)}) %reduce-scatter.15.cloned.1.call-update) | async-done | bytes 65552 | tf_op jit(solution)/shard_map/reduce_scatter | solution.py:286
  517.0 14.2 %all_gather.38 = bf16[4096,32]{0,1:T(8,128)(2,1)S(1)} all-gather(bf16[512,32]{0,1:T(8,128)(2,1)S(1)} %get-tuple-element.666), channel_id=1, replica_groups=mesh['fsdp'=8,'ctx'=2,'tp'=2] {'fsdp'}, dimensions={0}, use_global_device_ids=true | all-gather | bytes 294912 | tf_op jit(solution)/shard_map/all_gather | solution.py:171
  531.2 28.8 %multiply_convert_fusion.1 = (bf16[4096,1024]{1,0:T(8,128)(2,1)}, bf16[4096,1024]{1,0:T(8,128)(2,1)}, bf16[4096,1024]{1,0:T(8,128)(2,1)}) fusion(f32[1024,4096]{0,1:T(8,128)} %fusion.60, f32[4096,1024]{1,0:T(8,128)} %fusion.139, f32[4096,1024]{1,0:T(8,128)} %fusion.140, s32[1024]{0:T(1024)S(1)} %fusion.119, bf16[4096,32]{0,1:T(8,128)(2,1)S(1)} %all_gather.38, ...), kind=kOutput, calls=%fused_computation.66 | convolution fusion | flops 1682472960 | bytes 76320768 | tf_op jit(solution)/shard_map/dot_general | solution.py:268
  560.1 14.8 %fusion.141 = f32[4096,1024]{1,0:T(8,128)} fusion(bf16[4096,1024]{1,0:T(8,128)(2,1)} %get-tuple-element.623, bf16[1024,1024]{1,0:T(8,128)(2,1)S(1)} %copy-done.48), kind=kOutput, calls=%fused_computation.225 | convolution fusion | flops 8589934592 | bytes 27262976 | tf_op jit(solution)/shard_map/dot_general | solution.py:27
  574.9 17.5 %add_convert_fusion = bf16[4096,1024]{1,0:T(8,128)(2,1)} fusion(f32[4096,1024]{1,0:T(8,128)} %fusion.141, bf16[4096,1024]{1,0:T(8,128)(2,1)} %get-tuple-element.622, bf16[1024,1024]{1,0:T(8,128)(2,1)S(1)} %copy-done.47), kind=kOutput, calls=%fused_computation.65 | convolution fusion | flops 8598323200 | bytes 35651584 | tf_op jit(solution)/shard_map/dot_general | solution.py:27
  592.6 87.8 %reduce-scatter.11.cloned.1.call-done = bf16[512,1024]{1,0:T(8,128)(2,1)} async-done(((bf16[4096,1024]{1,0:T(8,128)(2,1)}), bf16[512,1024]{1,0:T(8,128)(2,1)}) %reduce-scatter.11.cloned.1.call-update) | async-done | bytes 1048592 | tf_op jit(solution)/shard_map/reduce_scatter | solution.py:289
  680.4 2.7 add_convert_fusion.2
  683.2 38.5 %all-reduce.8.cloned.1.call-done = bf16[512,1024]{1,0:T(8,128)(2,1)} async-done(((bf16[512,1024]{1,0:T(8,128)(2,1)}), bf16[512,1024]{1,0:T(8,128)(2,1)}) %all-reduce.8.cloned.1.call-update) | async-done | bytes 1048592 | tf_op jit(solution)/shard_map/psum | solution.py:305
  724.1 3.3 convolution_convert_fusion.6
  728.9 33.3 %while.37 = (s32[]{:T(128)}, f32[4,1024,64]{1,2,0:T(8,128)}, bf16[4,1024,64]{1,2,0:T(8,128)(2,1)S(1)}, bf16[4,1024,64]{1,2,0:T(8,128)(2,1)S(1)}, s32[1,512]{1,0:...) while((s32[]{:T(128)}, f32[4,1024,64]{1,2,0:T(8,128)}, ...), condition=%wide.region_23.24_spmd.clone.clone, body=%wide.region_21.23_spmd.clone.sunk.clone | while | flops 683801600 | bytes 38339760 | solution.py:340
  763.3 15.0 %convolution_convert_fusion = bf16[4096,1024]{1,0:T(8,128)(2,1)} fusion(bf16[4096,1024]{1,0:T(8,128)(2,1)} %get-tuple-element.624, bf16[1024,1024]{1,0:T(8,128)(2,1)} %all-gather.21.cloned.1.call-done), kind=kOutput, calls=%fused_computation.76 | convolution fusion | flops 8594128896 | bytes 18874368 | tf_op jit(solution)/shard_map/dot_general | solution.py:27
  778.4 15.0 %convert_bitcast_fusion.2 = bf16[1024,1024]{0,1:T(8,128)(2,1)} fusion(bf16[4096,1024]{1,0:T(8,128)(2,1)} %get-tuple-element.624, bf16[1,4096,1024]{2,1,0:T(8,128)(2,1)} %all-gather.31.cloned.1.call-done), kind=kOutput, calls=%fused_computation.102 | convolution fusion | flops 8590983168 | bytes 18874368 | tf_op jit(solution)/shard_map/dot_general | solution.py:21
  793.5 14.7 %convolution_convert_fusion.1 = bf16[1024,1024]{1,0:T(8,128)(2,1)} fusion(bf16[4096,1024]{1,0:T(8,128)(2,1)} %all-gather.15.cloned.1.call-done, bf16[4096,1024]{1,0:T(8,128)(2,1)} %get-tuple-element.622), kind=kOutput, calls=%fused_computation.111 | convolution fusion | flops 8590983168 | bytes 18874368 | tf_op jit(solution)/shard_map/dot_general | solution.py:21
  808.2 14.8 %convolution_convert_fusion.2 = bf16[1024,1024]{1,0:T(8,128)(2,1)} fusion(bf16[4096,1024]{1,0:T(8,128)(2,1)} %all-gather.15.cloned.1.call-done, bf16[4096,1024]{1,0:T(8,128)(2,1)} %get-tuple-element.623), kind=kOutput, calls=%fused_computation.112 | convolution fusion | flops 8590983168 | bytes 18874368 | tf_op jit(solution)/shard_map/dot_general | solution.py:21
  834.8 40.8 %reduce-scatter.13.cloned.1.call-done = bf16[512,1024]{1,0:T(8,128)(2,1)} async-done(((bf16[4096,1024]{1,0:T(8,128)(2,1)}), bf16[512,1024]{1,0:T(8,128)(2,1)}) %reduce-scatter.13.cloned.1.call-update) | async-done | bytes 1048592 | tf_op jit(solution)/shard_map/reduce_scatter | solution.py:294
  875.8 32.8 %reduce-scatter.23.cloned.1.call-done = bf16[1024,512]{0,1:T(8,128)(2,1)} async-done(((bf16[1024,1024]{0,1:T(8,128)(2,1)}), bf16[1024,512]{0,1:T(8,128)(2,1)}) %reduce-scatter.23.cloned.1.call-update) | async-done | bytes 1048592 | tf_op jit(solution)/shard_map/reduce_scatter | solution.py:99
  910.8 31.3 %all_to_all.31 = bf16[8,128,512]{2,1,0:T(8,128)(2,1)} all-to-all(bf16[8,128,512]{2,1,0:T(8,128)(2,1)} %bitcast.393), channel_id=1, replica_groups=mesh['fsdp'=8,'ctx'=2,'tp'=2] {'fsdp'}, dimensions={0} | all-to-all | bytes 2097152 | tf_op jit(solution)/shard_map/all_to_all | solution.py:103
  943.2 31.3 %all_to_all.32 = bf16[8,128,512]{2,1,0:T(8,128)(2,1)} all-to-all(bf16[8,128,512]{2,1,0:T(8,128)(2,1)} %bitcast.401), channel_id=1, replica_groups=mesh['fsdp'=8,'ctx'=2,'tp'=2] {'fsdp'}, dimensions={0} | all-to-all | bytes 2097152 | tf_op jit(solution)/shard_map/all_to_all | solution.py:103
  974.6 3.2 reduce-scatter.19.cloned.1.call-done
  977.7 31.3 %all_to_all.33 = bf16[8,128,512]{2,1,0:T(8,128)(2,1)} all-to-all(bf16[8,128,512]{2,1,0:T(8,128)(2,1)} %bitcast.400), channel_id=1, replica_groups=mesh['fsdp'=8,'ctx'=2,'tp'=2] {'fsdp'}, dimensions={0} | all-to-all | bytes 2097152 | tf_op jit(solution)/shard_map/all_to_all | solution.py:103
  1010.7 4.3 convolution_convert_fusion.4
  1015.0 2.7 convolution_convert_fusion.3
  1017.7 25.5 %all-reduce.12.cloned.1.call-done = (bf16[512,1024]{1,0:T(8,128)(2,1)}, bf16[512,1024]{1,0:T(8,128)(2,1)}) async-done(((bf16[512,1024]{1,0:T(8,128)(2,1)}, bf16[512,1024]{1,0:T(8,128)(2,1)}), (bf16[512,1024]{1,0:T(8,128)(2,1)}, bf16[512,1024]{1,0:T(8,128)(2,1)})) %all-reduce.12.cloned.1.call-update) | async-done | bytes 2097168 | tf_op jit(solution)/shard_map/psum | solution.py:312
  1045.1 17.5 %concatenate.88 = bf16[1024,1664]{0,1:T(8,128)(2,1)} concatenate(bf16[1024,1024]{0,1:T(8,128)(2,1)} %convolution_convert_fusion.3, bf16[1024,512]{0,1:T(8,128)(2,1)} %convolution_convert_fusion.4, bf16[1024,32]{0,1:T(8,128)(2,1)S(1)} %convolution_convert_fusion.8, bf16[1024,1]{0,1:T(2,128)(2,1)S(1)} %convert_element_type.321, bf16[1024,1]{0,1:T(2,128)(2,1)S(1)} %convert_element_type.324, ...), dimensions={1} | concatenate | bytes 6815744 | tf_op jit(solution)/shard_map/concatenate | solution.py:390
  1062.6 5.6 copy.131
  1068.3 9.4 all-gather.27.cloned.1.call-done
  1079.6 2.5 convert_bitcast_fusion
  1082.2 5.6 copy.128
  1087.8 24.6 %all-gather.25.cloned.1.call-done = bf16[8,128,1024]{2,1,0:T(8,128)(2,1)} async-done(((bf16[8,128,512]{2,1,0:T(8,128)(2,1)}), bf16[8,128,1024]{2,1,0:T(8,128)(2,1)}) %all-gather.25.cloned.1.call-update) | async-done | bytes 2097168 | tf_op jit(solution)/shard_map/all_gather | solution.py:106
  1114.3 2.5 convert.61
  1116.9 30.1 %all-gather.23.cloned.1.call-done = bf16[8,128,1024]{2,1,0:T(8,128)(2,1)} async-done(((bf16[8,128,512]{2,1,0:T(8,128)(2,1)}), bf16[8,128,1024]{2,1,0:T(8,128)(2,1)}) %all-gather.23.cloned.1.call-update) | async-done | bytes 2097168 | tf_op jit(solution)/shard_map/all_gather | solution.py:106
  1148.9 2.5 convert.60
  1152.0 39.9 %reduce-scatter.25.cloned.1.call-done = bf16[128,1664]{1,0:T(8,128)(2,1)} async-done(((bf16[1024,1664]{1,0:T(8,128)(2,1)}), bf16[128,1664]{1,0:T(8,128)(2,1)}) %reduce-scatter.25.cloned.1.call-update) | async-done | bytes 426000
  1193.9 4.4 fusion.75
  1198.5 16.3 %psum.46 = bf16[128,128]{0,1:T(8,128)(2,1)S(1)} all-reduce(bf16[128,128]{0,1:T(8,128)(2,1)S(1)} %copy.135), channel_id=1, replica_groups=mesh['fsdp'=8,'ctx'=2,'tp'=2] {'ctx','tp'}, use_global_device_ids=true, to_apply=%region_30.31 | all-reduce | flops 16384 | bytes 65536 | tf_op jit(solution)/shard_map/psum | solution.py:406
  1216.0 2.9 all-reduce.10.cloned.1.call-done
  (341 shorter events, 131.7 us)
Async XLA Ops:
  7.2 54.7 %all-gather.13.cloned.1.call-start = ((), (), s32[]{:S(2)}) async-start(), calls=%async_computation.14 | async-start | bytes 3833856 | tf_op jit(solution)/shard_map/all_gather | solution.py:142
  17.7 69.2 %all-gather.29.cloned.1.call-start = ((), (), s32[]{:S(2)}) async-start(), calls=%async_computation.32 | async-start | bytes 1572864 | tf_op jit(solution)/shard_map/all_gather | solution.py:197
  24.1 2.8 copy-start.41
  24.1 2.8 copy-start.1
  27.2 47.2 %copy-start.43 = (f32[512]{0:T(512)}, f32[512]{0:T(512)S(1)}, u32[]{:S(2)}) copy-start(f32[512]{0:T(512)S(1)} %add_rsqrt_fusion.1) | copy-start | bytes 6148
  28.2 47.1 %copy-start.24 = (f32[512,32]{0,1:T(8,128)}, f32[512,32]{0,1:T(8,128)S(1)}, u32[]{:S(2)}) copy-start(f32[512,32]{0,1:T(8,128)S(1)} %get-tuple-element.669) | copy-start | bytes 196612
  62.7 11.8 copy-start.37
  62.7 118.9 %copy-start.35 = (f32[1024,1]{0,1:T(1,128)}, f32[1024,1]{0,1:T(1,128)S(1)}, u32[]{:S(2)}) copy-start(f32[1024,1]{0,1:T(1,128)S(1)} %get-tuple-element.625) | copy-start | bytes 12292
  68.4 71.2 %all-to-all-start.2 = ((bf16[8,128,512]{2,1,0:T(8,128)(2,1)}), bf16[8,128,512]{2,1,0:T(8,128)(2,1)}, u32[]{:S(2)}, u32[]{:S(2)}) async-start(bf16[8,128,512]{2,1,0:T(8,128)(2,1)} %constant_dynamic-slice_fusion.1), calls=%async_computation.2 | async-start | bytes 2097152 | tf_op jit(solution)/shard_map/all_to_all | solution.py:94
  72.7 107.1 %all-reduce.6.cloned.1.call-start = ((), (), s32[]{:S(2)}) async-start(), calls=%async_computation.15 | async-start | bytes 2097152 | tf_op jit(solution)/shard_map/psum | solution.py:251
  132.1 7.5 copy-start.10
  132.1 7.5 copy-start.12
  132.1 7.5 copy-start.31
  132.1 7.5 copy-start.33
  139.6 80.4 %all-gather.21.cloned.1.call-start = ((), (), s32[]{:S(2)}) async-start(), calls=%async_computation.19 | async-start | bytes 3145728 | tf_op jit(solution)/shard_map/all_gather | solution.py:95
  140.2 157.9 %all-gather.31.cloned.1.call-start = ((), (), s32[]{:S(2)}) async-start(), calls=%async_computation.33 | async-start | bytes 9437184 | tf_op jit(solution)/shard_map/all_gather | solution.py:172
  140.8 191.0 %all-gather.19.cloned.1.call-start = ((), (), s32[]{:S(2)}) async-start(), calls=%async_computation.18 | async-start | bytes 3145728 | tf_op jit(solution)/shard_map/all_gather | solution.py:95
  176.4 239.7 %all-gather.15.cloned.1.call-start = ((), (), s32[]{:S(2)}) async-start(), calls=%async_computation.16 | async-start | bytes 9437184 | tf_op jit(solution)/shard_map/all_gather | solution.py:258
  187.2 31.2 %all-to-all-start = ((bf16[8,128,512]{1,2,0:T(8,128)(2,1)}), bf16[8,128,512]{1,2,0:T(8,128)(2,1)S(1)}, u32[]{:S(2)}, u32[]{:S(2)}) async-start(bf16[8,128,512]{1,2,0:T(8,128)(2,1)} %constant_dynamic-slice_fusion.3), calls=%async_computation | async-start | bytes 2097152 | tf_op jit(solution)/shard_map/all_to_all | solution.py:94
  191.8 258.1 %all-gather.17.cloned.1.call-start = ((), (), s32[]{:S(2)}) async-start(), calls=%async_computation.17 | async-start | bytes 3145728 | tf_op jit(solution)/shard_map/all_gather | solution.py:95
  219.8 296.4 %reduce-scatter.15.cloned.1.call-start = ((), (), s32[]{:S(2)}) async-start(), calls=%async_computation.22 | async-start | bytes 589824 | tf_op jit(solution)/shard_map/reduce_scatter | solution.py:286
  466.3 18.8 %copy-start.45 = (s32[1,512,8]{1,2,0:T(8,128)S(1)}, s32[1,512,8]{1,2,0:T(8,128)}, u32[]{:S(2)}) copy-start(s32[1,512,8]{1,2,0:T(8,128)} %param.20) | copy-start | bytes 49156
  466.3 18.9 %copy-start.6 = (bf16[512,1024]{1,0:T(8,128)(2,1)S(1)}, bf16[512,1024]{1,0:T(8,128)(2,1)}, u32[]{:S(2)}) copy-start(bf16[512,1024]{1,0:T(8,128)(2,1)} %multiply_convert_fusion.4) | copy-start | bytes 3145732
  485.1 195.3 %reduce-scatter.11.cloned.1.call-start = ((), (), s32[]{:S(2)}) async-start(), calls=%async_computation.20 | async-start | bytes 9437184 | tf_op jit(solution)/shard_map/reduce_scatter | solution.py:289
  531.2 28.8 %copy-start.48 = (bf16[1024,1024]{1,0:T(8,128)(2,1)S(1)}, bf16[1024,1024]{1,0:T(8,128)(2,1)}, u32[]{:S(2)}) copy-start(bf16[1024,1024]{1,0:T(8,128)(2,1)} %all-gather.17.cloned.1.call-done) | copy-start | bytes 6291460
  560.1 14.8 %copy-start.47 = (bf16[1024,1024]{1,0:T(8,128)(2,1)S(1)}, bf16[1024,1024]{1,0:T(8,128)(2,1)}, u32[]{:S(2)}) copy-start(bf16[1024,1024]{1,0:T(8,128)(2,1)} %all-gather.19.cloned.1.call-done) | copy-start | bytes 6291460
  592.4 90.7 %copy-start.9 = (bf16[4,1024,64]{1,2,0:T(8,128)(2,1)S(1)}, bf16[4,1024,64]{1,2,0:T(8,128)(2,1)}, u32[]{:S(2)}) copy-start(bf16[4,1024,64]{1,2,0:T(8,128)(2,1)} %copy-done.8) | copy-start | bytes 1572868
  592.4 129.3 %all-reduce.8.cloned.1.call-start = ((), (), s32[]{:S(2)}) async-start(), calls=%async_computation.23 | async-start | bytes 2097152 | tf_op jit(solution)/shard_map/psum | solution.py:305
  592.5 129.2 %copy-start.2 = (bf16[1,512,1024]{2,1,0:T(8,128)(2,1)S(1)}, bf16[1,512,1024]{2,1,0:T(8,128)(2,1)}, u32[]{:S(2)}) copy-start(bf16[1,512,1024]{2,1,0:T(8,128)(2,1)} %param.18) | copy-start | bytes 3145732
  592.5 129.2 %copy-start.4 = (bf16[512,1024]{1,0:T(8,128)(2,1)S(1)}, bf16[512,1024]{1,0:T(8,128)(2,1)}, u32[]{:S(2)}) copy-start(bf16[512,1024]{1,0:T(8,128)(2,1)} %all-reduce.6.cloned.1.call-done) | copy-start | bytes 3145732
  592.5 129.2 %copy-start.36 = (f32[1024,1]{0,1:T(1,128)S(1)}, f32[1024,1]{0,1:T(1,128)}, u32[]{:S(2)}) copy-start(f32[1024,1]{0,1:T(1,128)} %copy-done.35) | copy-start | bytes 12292
  592.5 129.2 %copy-start.40 = (f32[512]{0:T(512)S(1)}, f32[512]{0:T(512)}, u32[]{:S(2)}) copy-start(f32[512]{0:T(512)} %copy-done.39) | copy-start | bytes 6148
  683.1 146.3 %reduce-scatter.17.cloned.1.call-start = ((), (), s32[]{:S(2)}) async-start(), calls=%async_computation.24 | async-start | bytes 1572864 | tf_op jit(solution)/shard_map/reduce_scatter | solution.py:353
  724.1 286.6 %copy-start.46 = (f32[512]{0:T(512)}, f32[512]{0:T(512)S(1)}, u32[]{:S(2)}) copy-start(f32[512]{0:T(512)S(1)} %broadcast_multiply_fusion.1) | copy-start | bytes 6148
  724.1 4.8 copy-start.32
  724.1 4.8 copy-start.34
  724.1 4.8 copy-start.42
  729.1 2.6 copy-start.11
  729.1 2.6 copy-start.13
  737.4 2.6 copy-start.11
  737.4 2.6 copy-start.13
  745.7 2.6 copy-start.11
  745.7 2.6 copy-start.13
  753.9 2.6 copy-start.11
  753.9 2.6 copy-start.13
  763.3 112.4 %reduce-scatter.13.cloned.1.call-start = ((), (), s32[]{:S(2)}) async-start(), calls=%async_computation.21 | async-start | bytes 9437184 | tf_op jit(solution)/shard_map/reduce_scatter | solution.py:294
  778.4 130.2 %reduce-scatter.23.cloned.1.call-start = ((), (), s32[]{:S(2)}) async-start(), calls=%async_computation.30 | async-start | bytes 3145728 | tf_op jit(solution)/shard_map/reduce_scatter | solution.py:99
  793.4 149.8 %reduce-scatter.21.cloned.1.call-start = ((), (), s32[]{:S(2)}) async-start(), calls=%async_computation.28 | async-start | bytes 3145728 | tf_op jit(solution)/shard_map/reduce_scatter | solution.py:99
  808.2 169.5 %reduce-scatter.19.cloned.1.call-start = ((), (), s32[]{:S(2)}) async-start(), calls=%async_computation.26 | async-start | bytes 3145728 | tf_op jit(solution)/shard_map/reduce_scatter | solution.py:99
  823.1 220.1 %all-reduce.12.cloned.1.call-start = ((), (), s32[]{:S(2)}) async-start(), calls=%async_computation.35 | async-start | bytes 4194304 | tf_op jit(solution)/shard_map/psum | solution.py:312
  829.4 3.8 copy-start.17
  875.7 202.0 %all-gather.27.cloned.1.call-start = ((), (), s32[]{:S(2)}) async-start(), calls=%async_computation.31 | async-start | bytes 3145728 | tf_op jit(solution)/shard_map/all_gather | solution.py:106
  942.2 170.2 %all-gather.25.cloned.1.call-start = ((), (), s32[]{:S(2)}) async-start(), calls=%async_computation.29 | async-start | bytes 3145728 | tf_op jit(solution)/shard_map/all_gather | solution.py:106
  974.5 172.5 %all-gather.23.cloned.1.call-start = ((), (), s32[]{:S(2)}) async-start(), calls=%async_computation.27 | async-start | bytes 3145728 | tf_op jit(solution)/shard_map/all_gather | solution.py:106
  1009.1 182.9 %reduce-scatter.25.cloned.1.call-start = ((), (), s32[]{:S(2)}) async-start(), calls=%async_computation.34 | async-start | bytes 3833856
  1010.7 4.3 copy-start.23
  1010.7 4.3 copy-start.30
  1010.7 4.3 copy-start.38
  1010.7 4.3 copy-start.44
  1068.2 150.6 %all-reduce.10.cloned.1.call-start = ((), (), s32[]{:S(2)}) async-start(), calls=%async_computation.25 | async-start | bytes 786432 | tf_op jit(solution)/shard_map/psum | solution.py:405
  1148.9 45.0 %copy-start.19 = (bf16[1,512,1024]{2,1,0:T(8,128)(2,1)S(1)}, bf16[1,512,1024]{2,1,0:T(8,128)(2,1)}, u32[]{:S(2)}) copy-start(bf16[1,512,1024]{2,1,0:T(8,128)(2,1)} %param.31) | copy-start | bytes 3145732
  1151.4 42.5 %copy-start.5 = (bf16[512,1024]{1,0:T(8,128)(2,1)S(1)}, bf16[512,1024]{1,0:T(8,128)(2,1)}, u32[]{:S(2)}) copy-start(bf16[512,1024]{1,0:T(8,128)(2,1)} %all-reduce.6.cloned.1.call-done) | copy-start | bytes 3145732
  1193.9 4.5 slice-start.1
  1218.9 3.6 copy-start.21
  (20 other events, 33.0 us)
Sparse Core Ops, SparseCore 0:
  17.8 44.0 all-gather.12
  67.3 19.5 all-gather.28
  139.7 40.0 all-reduce.5
  181.3 33.1 all-gather.20
  215.9 82.0 all-gather.30
  300.1 31.6 all-gather.18
  334.0 82.0 all-gather.14
  418.3 31.6 all-gather.16
  485.2 30.9 reduce-scatter.14
  592.5 87.8 reduce-scatter.10
  683.3 38.4 all-reduce.7
  763.4 20.3 reduce-scatter.16
  786.0 89.5 reduce-scatter.12
  878.4 30.1 reduce-scatter.22
  911.3 31.8 reduce-scatter.20
  945.9 31.8 reduce-scatter.18
  980.1 63.0 all-reduce.11
  1044.6 33.1 all-gather.26
  1079.3 33.1 all-gather.24
  1113.8 33.1 all-gather.22
  1149.3 42.5 reduce-scatter.24
  1194.2 24.5 all-reduce.9

commit v2 on v1

--- a/solution.py
+++ b/solution.py
@@ -97,7 +97,7 @@
 
 def return_experts(grad, groups, units):
     summed = lax.psum_scatter(
-        grad.astype(jnp.bfloat16), "ctx", scatter_dimension=1, tiled=True
+        grad, "ctx", scatter_dimension=1, tiled=True
     )
     depth = summed.shape[0] // groups
     moved = lax.all_to_all(
@@ -139,6 +139,10 @@
     q_cols, k_cols, o_cols = w_query.shape[1], w_key.shape[1], w_output.shape[0]
     small_at = q_cols + 2 * k_cols + o_cols
     shard_rows = w_query.shape[0]
+    token_ids = expert_ids.reshape(tok_count, TOPK)
+    route_mask = jnp.sum(
+        (token_ids[:, :, None] == jnp.arange(E, dtype=jnp.int32)).astype(jnp.float32), axis=1
+    )
     packed_w = lax.all_gather(
         jnp.concatenate(
             [
@@ -150,6 +154,7 @@
                 norm1_gain[:, None],
                 norm2_gain[:, None],
                 jnp.zeros((shard_rows, 128 - E - 2), jnp.bfloat16),
+                route_mask.astype(jnp.bfloat16).reshape(shard_rows, -1),
             ],
             axis=1,
         ),
@@ -164,11 +169,7 @@
     router_w = packed_w[:, small_at : small_at + E]
     gain_one = packed_w[:, small_at + E]
     gain_two = packed_w[:, small_at + E + 1]
-    token_ids = expert_ids.reshape(tok_count, TOPK)
-    route_mask = jnp.sum(
-        (token_ids[:, :, None] == jnp.arange(E, dtype=jnp.int32)).astype(jnp.float32), axis=1
-    )
-    mask_all = lax.all_gather(route_mask.astype(jnp.bfloat16), "fsdp", axis=0, tiled=True)
+    mask_all = packed_w[:, small_at + 128 :].reshape(-1, E)
     grad_all = lax.all_gather(
         cotangent.reshape(tok_count, model_width), "fsdp", axis=0, tiled=True
     )
@@ -255,7 +256,8 @@
     normed_two = resid * factor_two
     second_in = (normed_two * gain_two.astype(jnp.float32)).astype(jnp.bfloat16)
     router = router_probs(second_in, router_w)
-    normed_all = lax.all_gather(second_in, "fsdp", axis=0, tiled=True)
+    ready_in = lax.optimization_barrier((second_in, grad_all, down_wt, gate_w, up_w))[0]
+    normed_all = lax.all_gather(ready_in, "fsdp", axis=0, tiled=True)
     columns = gate_w.shape[1]
     column_expert = lax.axis_index("fsdp") * (columns // hidden_units) + (
         jnp.arange(columns, dtype=jnp.int32) // hidden_units
@@ -282,21 +284,34 @@
     gate_grad_all = contract_cols(
         (hidden * grad_mid).astype(jnp.bfloat16), owner.astype(jnp.bfloat16)
     )
-    grad_route = (
-        lax.psum_scatter(gate_grad_all, "fsdp", scatter_dimension=0, tiled=True) * route_mask
-    )
     grad_rows = contract_cols(grad_gate_pre, gate_w) + contract_cols(grad_up_pre, up_w)
-    grad_in_part = lax.psum_scatter(
-        grad_rows.astype(jnp.bfloat16), "fsdp", scatter_dimension=0, tiled=True
-    )
-    moe_rows = contract_cols(weighted, down_wt).astype(jnp.bfloat16)
-    moe_rows, _ = lax.optimization_barrier((moe_rows, grad_in_part))
+    arrived = lax.psum_scatter(
+        jnp.concatenate(
+            [
+                grad_rows.astype(jnp.bfloat16),
+                gate_grad_all.astype(jnp.bfloat16),
+                jnp.zeros((grad_rows.shape[0], 128 - E), jnp.bfloat16),
+            ],
+            axis=1,
+        ),
+        "fsdp",
+        scatter_dimension=0,
+        tiled=True,
+    )
+    gate_grad_w = contract_rows(normed_all, grad_gate_pre).astype(jnp.bfloat16)
+    up_grad_w = contract_rows(normed_all, grad_up_pre).astype(jnp.bfloat16)
+    down_grad_w = contract_rows(grad_all, weighted).astype(jnp.bfloat16)
+    moe_made = contract_cols(weighted, down_wt).astype(jnp.bfloat16)
+    moe_rows = lax.optimization_barrier((moe_made, arrived))[0]
+    settled = lax.optimization_barrier(
+        (arrived, gate_grad_w, up_grad_w, down_grad_w, moe_made)
+    )[0]
+    grad_in_part = settled[:, :model_width]
+    grad_route = settled[:, model_width : model_width + E].astype(jnp.float32) * route_mask
     moe_part = lax.psum_scatter(moe_rows, "fsdp", scatter_dimension=0, tiled=True)
-    gate_part = return_experts(contract_rows(normed_all, grad_gate_pre), groups, hidden_units)
-    up_part = return_experts(contract_rows(normed_all, grad_up_pre), groups, hidden_units)
-    down_part = return_experts(
-        contract_rows(grad_all, weighted), groups, hidden_units
-    ).transpose(0, 2, 1)
+    gate_part = return_experts(gate_grad_w, groups, hidden_units)
+    up_part = return_experts(up_grad_w, groups, hidden_units)
+    down_part = return_experts(down_grad_w, groups, hidden_units).transpose(0, 2, 1)
     grad_out = cotangent.reshape(tok_count, model_width).astype(jnp.float32)
     grad_logits = (
         router * (grad_route - jnp.sum(router * grad_route, axis=-1, keepdims=True))

time: 1240 us -> 1230 us (level)
  waiting for transfers between devices: 634 us -> 600 us
  blocking collectives: 155 us -> 171 us
  local copies, waits for them, and re-layouts: 109 us -> 124 us
    reduce_scatter x5 -> x4, waiting for transfers between devices: 148 us -> 74.9 us  [the longest x3 39.2 us: return_experts(): summed = lax.psum_scatter(grad, 'ctx', scatter_dimension=1, tiled=True)]
    reduce_scatter x1, waiting for transfers between devices: 40.8 us -> 85.5 us  [body(): lax.psum_scatter(moe_rows, 'fsdp', scatter_dimension=0, tiled=True)]
    all_gather x3, waiting for transfers between devices: 35.4 us -> 66.1 us  [gather_experts(): return lax.all_gather(moved.reshape(-1, part), 'ctx', axis=1, tiled=True)]
    all_to_all x1 -> x2, blocking collectives: 31 us -> 60.7 us  [gather_experts(): lax.all_to_all(mine, 'fsdp', split_axis=0, concat_axis=0, tiled=True)]
    all_to_all x2 -> x1, waiting for transfers between devices: 26.5 us -> 0.01 us  [gather_experts(): lax.all_to_all(mine, 'fsdp', split_axis=0, concat_axis=0, tiled=True)]
    dot_general x17, matrix products: 80.7 us -> 58.8 us  [matmul(): return jnp.dot(left, right, preferred_element_type=jnp.float32)]
    all_gather x1, waiting for transfers between devices: 84.4 us -> 66.2 us  [body(): normed_all = lax.all_gather(ready_in, 'fsdp', axis=0, tiled=True)]
    all_gather x1 -> x0, blocking collectives: 14.2 us -> none  [body(): lax.all_gather(route_mask.astype(jnp.bfloat16), 'fsdp', axis=0, tiled=True)]
  transfers between devices with their start and end apart: 24 -> 22, of which waited for: 21 -> 18; matrix products, arithmetic and copies ran while one was open for 20% -> 18% of each run, Pallas kernels for 0% -> 0%
where the time goes in v2:
time: 1230 us; the launch traced here: 1220 us
  waiting for transfers between devices  600 us (49%)
  matrix products  255 us (21%)
  blocking collectives  171 us (14%)
  local copies, waits for them, and re-layouts  124 us (10%)
  other arithmetic  47.9 us (4%)
  between operations  15.5 us (1%)
    dot_general x21, matrix products, contract_cols(): lax.dot_general(left, right, (((1,), (1,)), ((), ())), preferred_element_...  106 us
    all_to_all x3, blocking collectives, return_experts(): lax.all_to_all(summed.reshape(groups, depth, -1), 'fsdp', split_axis=0, c...  94.1 us
    reduce_scatter x1, waiting for transfers between devices, body(): lax.psum_scatter(moe_rows, 'fsdp', scatter_dimension=0, tiled=True)  85.5 us
    all_gather x1, waiting for transfers between devices, body(): lax.all_gather(cotangent.reshape(tok_count, model_width), 'fsdp', axis=0,...  80.8 us
    all_gather x3, waiting for transfers between devices, return_experts(): lax.all_gather(moved, 'ctx', axis=2, tiled=True)  69.9 us
    all_gather x1, waiting for transfers between devices, body(): normed_all = lax.all_gather(ready_in, 'fsdp', axis=0, tiled=True)  66.2 us
    all_gather x3, waiting for transfers between devices, gather_experts(): return lax.all_gather(moved.reshape(-1, part), 'ctx', axis=1, tiled=True)  66.1 us
    dot_general x14, matrix products, contract_rows(): lax.dot_general(left, right, (((0,), (0,)), ((), ())), preferred_element_...  61.2 us
  transfers between devices with their start and end apart: 22, of which 18 were waited for; matrix products, arithmetic and copies ran while one was open for 18% of the time, Pallas kernels for 0%

profile of v2, /device:TPU:0, one launch (start us, length us, event | category | flops | bytes accessed | tf_op | source)
XLA Modules:
  0.0 1218.9 jit_solution(8506057984332883868)
XLA Ops:
  12.1 8.1 concatenate.76
  22.7 3.6 copy.178
  27.7 38.9 %all-gather.13.cloned.1.call-done = bf16[1024,1792]{0,1:T(8,128)(2,1)} async-done(((bf16[128,1792]{0,1:T(8,128)(2,1)}), bf16[1024,1792]{0,1:T(8,128)(2,1)}) %all-gather.13.cloned.1.call-update) | async-done | bytes 3670032 | tf_op jit(solution)/shard_map/all_gather | solution.py:146
  72.9 4.2 all-to-all-start.1
  80.4 11.1 all-gather.29.cloned.1.call-done
  97.7 2.4 copy.216
  100.1 24.7 %while.36 = (s32[]{:T(128)}, bf16[4,1024,64]{1,2,0:T(8,128)(2,1)}, f32[4,1024]{1,0:T(4,128)}, s32[1,512]{1,0:T(1,128)S(1)}, s32[1,1024]{1,0:T(1,128)S(1)}, /*ind...) while((s32[]{:T(128)}, bf16[4,1024,64]{1,2,0:T(8,128)(2,1)}, ...), condition=%wide.region_7.8_spmd.clone.clone, body=%wide.region_4.7_spmd.clone.sunk.clone | while | flops 279968768 | bytes 17909920 | solution.py:245
  124.8 2.6 convert_element_type.300
  129.3 3.0 convolution_convert_fusion.5
  134.7 3.2 copy.180
  138.0 31.0 %all_to_all.30 = bf16[8,128,512]{1,2,0:T(8,128)(2,1)S(1)} all-to-all(bf16[8,128,512]{1,2,0:T(8,128)(2,1)S(1)} %constant_dynamic-slice_fusion.1), channel_id=1, replica_groups=mesh['fsdp'=8,'ctx'=2,'tp'=2] {'fsdp'}, dimensions={0} | all-to-all | bytes 2097152 | tf_op jit(solution)/shard_map/all_to_all | solution.py:94
  170.4 3.1 copy.177
  173.5 2.7 reshape.525
  177.5 29.7 %all_to_all.31 = bf16[8,128,512]{2,1,0:T(8,128)(2,1)} all-to-all(bf16[8,128,512]{2,1,0:T(8,128)(2,1)S(1)} %constant_dynamic-slice_fusion.3), channel_id=1, replica_groups=mesh['fsdp'=8,'ctx'=2,'tp'=2] {'fsdp'}, dimensions={0} | all-to-all | bytes 2097152 | tf_op jit(solution)/shard_map/all_to_all | solution.py:94
  211.5 31.5 %all-gather.19.cloned.1.call-done = bf16[1024,1024]{1,0:T(8,128)(2,1)} async-done(((bf16[1024,512]{1,0:T(8,128)(2,1)}), bf16[1024,1024]{1,0:T(8,128)(2,1)}) %all-gather.19.cloned.1.call-update) | async-done | bytes 2097168 | tf_op jit(solution)/shard_map/all_gather | solution.py:95
  242.9 34.6 %all-gather.15.cloned.1.call-done = bf16[1024,1024]{1,0:T(8,128)(2,1)} async-done(((bf16[1024,512]{1,0:T(8,128)(2,1)}), bf16[1024,1024]{1,0:T(8,128)(2,1)}) %all-gather.15.cloned.1.call-update) | async-done | bytes 2097168 | tf_op jit(solution)/shard_map/all_gather | solution.py:95
  280.6 80.8 %all-gather.31.cloned.1.call-done = bf16[1,4096,1024]{2,1,0:T(8,128)(2,1)} async-done(((bf16[1,512,1024]{2,1,0:T(8,128)(2,1)}), bf16[1,4096,1024]{2,1,0:T(8,128)(2,1)}) %all-gather.31.cloned.1.call-update) | async-done | bytes 8388624 | tf_op jit(solution)/shard_map/all_gather | solution.py:173
  361.3 16.1 %fusion.122 = f32[1024,4096]{0,1:T(8,128)} fusion(bf16[1024,1024]{1,0:T(8,128)(2,1)} %all-gather.15.cloned.1.call-done, bf16[1,4096,1024]{2,1,0:T(8,128)(2,1)} %all-gather.31.cloned.1.call-done), kind=kOutput, calls=%fused_computation.210 | convolution fusion | flops 8589934592 | bytes 27262976 | tf_op jit(solution)/shard_map/dot_general | solution.py:17
  377.4 66.2 %all-gather.21.cloned.1.call-done = bf16[4096,1024]{0,1:T(8,128)(2,1)} async-done(((bf16[512,1024]{0,1:T(8,128)(2,1)}), bf16[4096,1024]{0,1:T(8,128)(2,1)}) %all-gather.21.cloned.1.call-update) | async-done | bytes 8388624 | tf_op jit(solution)/shard_map/all_gather | solution.py:260
  443.6 5.1 fusion.136
  450.0 11.5 fusion.139
  461.6 11.5 fusion.138
  473.1 28.4 %fusion.59 = bf16[4096,32]{0,1:T(8,128)(2,1)S(1)} fusion(f32[1024,4096]{0,1:T(8,128)} %fusion.122, f32[4096,1024]{1,0:T(8,128)} %fusion.139, s32[1024]{0:T(1024)S(1)} %fusion.115, f32[4096,1024]{1,0:T(8,128)} %fusion.138), kind=kOutput, calls=%fused_computation.75 | convolution fusion | flops 298024960 | bytes 50597888 | tf_op jit(solution)/shard_map/dot_general | solution.py:27
  501.5 28.7 %multiply_convert_fusion.1 = (bf16[4096,1024]{1,0:T(8,128)(2,1)}, bf16[4096,1024]{1,0:T(8,128)(2,1)}, bf16[4096,1024]{1,0:T(8,128)(2,1)}) fusion(f32[1024,4096]{0,1:T(8,128)} %fusion.122, f32[4096,1024]{1,0:T(8,128)} %fusion.138, f32[4096,1024]{1,0:T(8,128)} %fusion.139, s32[1024]{0:T(1024)S(1)} %fusion.115, f32[4096,32]{0,1:T(8,128)S(1)} %copy.183, ...), kind=kOutput, calls=%fused_computation.66 | convolution fusion | flops 1682341888 | bytes 76582912 | tf_op jit(solution)/shard_map/dot_general | solution.py:270
  530.2 14.5 %fusion.140 = f32[4096,1024]{0,1:T(8,128)} fusion(bf16[4096,1024]{1,0:T(8,128)(2,1)} %get-tuple-element.658, bf16[1024,1024]{1,0:T(8,128)(2,1)S(1)} %copy-done.53), kind=kOutput, calls=%fused_computation.227 | convolution fusion | flops 8589934592 | bytes 27262976 | tf_op jit(solution)/shard_map/dot_general | solution.py:27
  544.6 15.4 %add_convert_fusion = bf16[4096,1024]{0,1:T(8,128)(2,1)S(1)} fusion(f32[4096,1024]{0,1:T(8,128)} %fusion.140, bf16[4096,1024]{1,0:T(8,128)(2,1)} %get-tuple-element.657, bf16[1024,1024]{1,0:T(8,128)(2,1)} %all-gather.19.cloned.1.call-done), kind=kOutput, calls=%fused_computation.65 | convolution fusion | flops 8598323200 | bytes 35651584 | tf_op jit(solution)/shard_map/dot_general | solution.py:27
  560.1 6.9 maximum_maximum_fusion
  569.4 16.2 %convert_bitcast_fusion.2 = bf16[1024,1024]{0,1:T(8,128)(2,1)} fusion(bf16[4096,1024]{1,0:T(8,128)(2,1)} %get-tuple-element.659, bf16[1,4096,1024]{2,1,0:T(8,128)(2,1)} %all-gather.31.cloned.1.call-done), kind=kOutput, calls=%fused_computation.106 | convolution fusion | flops 8590983168 | bytes 18874368 | tf_op jit(solution)/shard_map/dot_general | solution.py:21
  585.6 14.4 %convolution_convert_fusion = bf16[4096,1024]{0,1:T(8,128)(2,1)} fusion(bf16[4096,1024]{1,0:T(8,128)(2,1)} %get-tuple-element.659, bf16[1024,1024]{1,0:T(8,128)(2,1)S(1)} %copy-done.54), kind=kOutput, calls=%fused_computation.73 | convolution fusion | flops 8594128896 | bytes 18874368 | tf_op jit(solution)/shard_map/dot_general | solution.py:27
  600.0 14.7 %convolution_convert_fusion.1 = bf16[1024,1024]{1,0:T(8,128)(2,1)} fusion(bf16[4096,1024]{0,1:T(8,128)(2,1)} %all-gather.21.cloned.1.call-done, bf16[4096,1024]{1,0:T(8,128)(2,1)} %get-tuple-element.657), kind=kOutput, calls=%fused_computation.109 | convolution fusion | flops 8590983168 | bytes 18874368 | tf_op jit(solution)/shard_map/dot_general | solution.py:21
  614.7 14.9 %convolution_convert_fusion.2 = bf16[1024,1024]{1,0:T(8,128)(2,1)} fusion(bf16[4096,1024]{0,1:T(8,128)(2,1)} %all-gather.21.cloned.1.call-done, bf16[4096,1024]{1,0:T(8,128)(2,1)} %get-tuple-element.658), kind=kOutput, calls=%fused_computation.110 | convolution fusion | flops 8590983168 | bytes 18874368 | tf_op jit(solution)/shard_map/dot_general | solution.py:21
  629.6 35.6 %reduce-scatter.10.cloned.1.call-done = bf16[512,1152]{0,1:T(8,128)(2,1)} async-done(((bf16[4096,1152]{0,1:T(8,128)(2,1)}), bf16[512,1152]{0,1:T(8,128)(2,1)}) %reduce-scatter.10.cloned.1.call-update) | async-done | bytes 1179664 | tf_op jit(solution)/shard_map/reduce_scatter | solution.py:288
  666.1 2.7 add_convert_fusion.2
  669.0 2.4 copy.187
  671.4 36.0 %all-reduce.8.cloned.1.call-done = bf16[512,1024]{0,1:T(8,128)(2,1)} async-done(((bf16[512,1024]{0,1:T(8,128)(2,1)}), bf16[512,1024]{0,1:T(8,128)(2,1)}) %all-reduce.8.cloned.1.call-update) | async-done | bytes 1048592 | tf_op jit(solution)/shard_map/psum | solution.py:320
  707.4 3.0 multiply_reduce_fusion.1
  710.4 3.1 convolution_convert_fusion.6
  715.1 32.9 %while.37 = (s32[]{:T(128)}, f32[4,1024,64]{1,2,0:T(8,128)}, bf16[4,1024,64]{1,2,0:T(8,128)(2,1)S(1)}, bf16[4,1024,64]{1,2,0:T(8,128)(2,1)S(1)}, s32[1,512]{1,0:...) while((s32[]{:T(128)}, f32[4,1024,64]{1,2,0:T(8,128)}, ...), condition=%wide.region_22.23_spmd.clone.clone, body=%wide.region_20.22_spmd.clone.sunk.clone | while | flops 683801600 | bytes 38339768 | solution.py:355
  758.4 11.2 reduce-scatter.14.cloned.1.call-done
  775.9 85.5 %reduce-scatter.12.cloned.1.call-done = bf16[512,1024]{0,1:T(8,128)(2,1)} async-done(((bf16[4096,1024]{0,1:T(8,128)(2,1)}), bf16[512,1024]{0,1:T(8,128)(2,1)}) %reduce-scatter.12.cloned.1.call-update) | async-done | bytes 1048592 | tf_op jit(solution)/shard_map/reduce_scatter | solution.py:311
  861.5 33.1 %reduce-scatter.16.cloned.1.call-done = bf16[1024,512]{1,0:T(8,128)(2,1)} async-done(((bf16[1024,1024]{1,0:T(8,128)(2,1)}), bf16[1024,512]{1,0:T(8,128)(2,1)}) %reduce-scatter.16.cloned.1.call-update) | async-done | bytes 1048592 | tf_op jit(solution)/shard_map/reduce_scatter | solution.py:99
  894.6 31.3 %all_to_all.32 = bf16[8,128,512]{2,1,0:T(8,128)(2,1)} all-to-all(bf16[8,128,512]{2,1,0:T(8,128)(2,1)} %bitcast.402), channel_id=1, replica_groups=mesh['fsdp'=8,'ctx'=2,'tp'=2] {'fsdp'}, dimensions={0} | all-to-all | bytes 2097152 | tf_op jit(solution)/shard_map/all_to_all | solution.py:103
  926.0 3.2 reduce-scatter.18.cloned.1.call-done
  929.2 31.5 %all_to_all.33 = bf16[8,128,512]{2,1,0:T(8,128)(2,1)} all-to-all(bf16[8,128,512]{2,1,0:T(8,128)(2,1)} %bitcast.401), channel_id=1, replica_groups=mesh['fsdp'=8,'ctx'=2,'tp'=2] {'fsdp'}, dimensions={0} | all-to-all | bytes 2097152 | tf_op jit(solution)/shard_map/all_to_all | solution.py:103
  960.7 3.0 reduce-scatter.20.cloned.1.call-done
  963.8 2.3 copy.213
  966.0 31.3 %all_to_all.34 = bf16[8,128,512]{2,1,0:T(8,128)(2,1)} all-to-all(bf16[8,128,512]{2,1,0:T(8,128)(2,1)} %bitcast.394), channel_id=1, replica_groups=mesh['fsdp'=8,'ctx'=2,'tp'=2] {'fsdp'}, dimensions={0} | all-to-all | bytes 2097152 | tf_op jit(solution)/shard_map/all_to_all | solution.py:103
  997.4 2.3 convolution_convert_fusion.8
  1000.5 4.2 convolution_convert_fusion.4
  1004.7 2.7 convolution_convert_fusion.3
  1007.4 22.3 %all-reduce.12.cloned.1.call-done = (bf16[512,1024]{0,1:T(8,128)(2,1)}, bf16[512,1024]{0,1:T(8,128)(2,1)}) async-done(((bf16[512,1024]{0,1:T(8,128)(2,1)}, bf16[512,1024]{0,1:T(8,128)(2,1)}), (bf16[512,1024]{0,1:T(8,128)(2,1)}, bf16[512,1024]{0,1:T(8,128)(2,1)})) %all-reduce.12.cloned.1.call-update) | async-done | bytes 2097168 | tf_op jit(solution)/shard_map/psum | solution.py:327
  1031.7 17.5 %concatenate.92 = bf16[1024,1664]{0,1:T(8,128)(2,1)} concatenate(bf16[1024,1024]{0,1:T(8,128)(2,1)} %convolution_convert_fusion.3, bf16[1024,512]{0,1:T(8,128)(2,1)} %convolution_convert_fusion.4, bf16[1024,32]{0,1:T(8,128)(2,1)S(1)} %copy-done.34, bf16[1024,1]{0,1:T(2,128)(2,1)S(1)} %convert_element_type.342, bf16[1024,1]{0,1:T(2,128)(2,1)S(1)} %convert_element_type.345, ...), dimensions={1} | concatenate | bytes 6815744 | tf_op jit(solution)/shard_map/concatenate | solution.py:405
  1049.2 5.6 copy.214
  1054.9 9.4 all-gather.23.cloned.1.call-done
  1066.2 2.5 convert.61
  1068.8 30.2 %all-gather.25.cloned.1.call-done = bf16[8,128,1024]{2,1,0:T(8,128)(2,1)} async-done(((bf16[8,128,512]{2,1,0:T(8,128)(2,1)}), bf16[8,128,1024]{2,1,0:T(8,128)(2,1)}) %all-gather.25.cloned.1.call-update) | async-done | bytes 2097168 | tf_op jit(solution)/shard_map/all_gather | solution.py:106
  1100.8 2.5 convert.62
  1103.4 30.3 %all-gather.27.cloned.1.call-done = bf16[8,128,1024]{2,1,0:T(8,128)(2,1)} async-done(((bf16[8,128,512]{2,1,0:T(8,128)(2,1)}), bf16[8,128,1024]{2,1,0:T(8,128)(2,1)}) %all-gather.27.cloned.1.call-update) | async-done | bytes 2097168 | tf_op jit(solution)/shard_map/all_gather | solution.py:106
  1135.6 2.5 convert_bitcast_fusion
  1138.1 5.7 copy.201
  1144.4 34.2 %reduce-scatter.22.cloned.1.call-done = bf16[128,1664]{1,0:T(8,128)(2,1)} async-done(((bf16[1024,1664]{1,0:T(8,128)(2,1)}), bf16[128,1664]{1,0:T(8,128)(2,1)}) %reduce-scatter.22.cloned.1.call-update) | async-done | bytes 426000
  1180.6 4.2 fusion.74
  1184.8 3.0 copy.197
  1189.2 16.4 %psum.46 = bf16[128,128]{0,1:T(8,128)(2,1)S(1)} all-reduce(bf16[128,128]{0,1:T(8,128)(2,1)S(1)} %copy.218), channel_id=1, replica_groups=mesh['fsdp'=8,'ctx'=2,'tp'=2] {'ctx','tp'}, use_global_device_ids=true, to_apply=%region_29.30 | all-reduce | flops 16384 | bytes 65536 | tf_op jit(solution)/shard_map/psum | solution.py:421
  (370 shorter events, 137.1 us)
Async XLA Ops:
  7.2 13.1 %copy-start.45 = (s32[1,1024]{1,0:T(1,128)S(1)}, s32[1,1024]{1,0:T(1,128)}, u32[]{:S(2)}) copy-start(s32[1,1024]{1,0:T(1,128)} %param.19) | copy-start | bytes 12292
  7.2 15.0 %copy-start.30 = (bf16[1,512,1024]{2,1,0:T(8,128)(2,1)S(1)}, bf16[1,512,1024]{2,1,0:T(8,128)(2,1)}, u32[]{:S(2)}) copy-start(bf16[1,512,1024]{2,1,0:T(8,128)(2,1)} %param.18) | copy-start | bytes 3145732
  7.2 59.3 %all-gather.13.cloned.1.call-start = ((), (), s32[]{:S(2)}) async-start(), calls=%async_computation.13 | async-start | bytes 4128768 | tf_op jit(solution)/shard_map/all_gather | solution.py:146
  20.2 71.4 %all-gather.29.cloned.1.call-start = ((), (), s32[]{:S(2)}) async-start(), calls=%async_computation.30 | async-start | bytes 1572864 | tf_op jit(solution)/shard_map/all_gather | solution.py:198
  22.7 187.4 %copy-start = (bf16[1,512,1024]{1,2,0:T(8,128)(2,1)}, bf16[1,512,1024]{1,2,0:T(8,128)(2,1)S(1)}, u32[]{:S(2)}) copy-start(bf16[1,512,1024]{1,2,0:T(8,128)(2,1)S(1)} %copy.164) | copy-start | bytes 3145732
  26.7 52.2 %copy-start.47 = (f32[512]{0:T(512)}, f32[512]{0:T(512)S(1)}, u32[]{:S(2)}) copy-start(f32[512]{0:T(512)S(1)} %add_rsqrt_fusion.1) | copy-start | bytes 6148
  27.7 52.1 %copy-start.26 = (f32[512,32]{0,1:T(8,128)}, f32[512,32]{0,1:T(8,128)S(1)}, u32[]{:S(2)}) copy-start(f32[512,32]{0,1:T(8,128)S(1)} %get-tuple-element.703) | copy-start | bytes 196612
  67.3 11.6 copy-start.41
  67.4 142.7 %copy-start.39 = (f32[1024,1]{0,1:T(1,128)}, f32[1024,1]{0,1:T(1,128)S(1)}, u32[]{:S(2)}) copy-start(f32[1024,1]{0,1:T(1,128)S(1)} %get-tuple-element.660) | copy-start | bytes 12292
  72.9 59.5 %all-to-all-start.1 = ((bf16[8,128,512]{1,2,0:T(8,128)(2,1)}), bf16[8,128,512]{1,2,0:T(8,128)(2,1)}, u32[]{:S(2)}, u32[]{:S(2)}) async-start(bf16[8,128,512]{1,2,0:T(8,128)(2,1)} %constant_dynamic-slice_fusion.2), calls=%async_computation.1 | async-start | bytes 2097152 | tf_op jit(solution)/shard_map/all_to_all | solution.py:94
  77.2 131.2 %all-reduce.6.cloned.1.call-start = ((), (), s32[]{:S(2)}) async-start(), calls=%async_computation.14 | async-start | bytes 2097152 | tf_op jit(solution)/shard_map/psum | solution.py:252
  124.8 7.5 copy-start.10
  124.8 7.5 copy-start.12
  124.8 7.5 copy-start.35
  124.8 7.5 copy-start.37
  132.3 79.1 %all-gather.17.cloned.1.call-start = ((), (), s32[]{:S(2)}) async-start(), calls=%async_computation.16 | async-start | bytes 3145728 | tf_op jit(solution)/shard_map/all_gather | solution.py:95
  134.7 108.2 %all-gather.19.cloned.1.call-start = ((), (), s32[]{:S(2)}) async-start(), calls=%async_computation.17 | async-start | bytes 3145728 | tf_op jit(solution)/shard_map/all_gather | solution.py:95
  170.4 107.2 %all-gather.15.cloned.1.call-start = ((), (), s32[]{:S(2)}) async-start(), calls=%async_computation.15 | async-start | bytes 3145728 | tf_op jit(solution)/shard_map/all_gather | solution.py:95
  207.3 154.1 %all-gather.31.cloned.1.call-start = ((), (), s32[]{:S(2)}) async-start(), calls=%async_computation.31 | async-start | bytes 9437184 | tf_op jit(solution)/shard_map/all_gather | solution.py:173
  208.0 235.6 %all-gather.21.cloned.1.call-start = ((), (), s32[]{:S(2)}) async-start(), calls=%async_computation.18 | async-start | bytes 9437184 | tf_op jit(solution)/shard_map/all_gather | solution.py:260
  210.1 67.5 %copy-start.43 = (f32[512]{0:T(512)}, f32[512]{0:T(512)S(1)}, u32[]{:S(2)}) copy-start(f32[512]{0:T(512)S(1)} %add_rsqrt_fusion) | copy-start | bytes 6148
  277.6 387.7 %reduce-scatter.10.cloned.1.call-start = ((), (), s32[]{:S(2)}) async-start(), calls=%async_computation.19 | async-start | bytes 10616832 | tf_op jit(solution)/shard_map/reduce_scatter | solution.py:288
  443.6 5.8 copy-start.2
  443.6 6.4 copy-start.55
  450.0 11.5 copy-start.52
  501.5 28.7 %copy-start.53 = (bf16[1024,1024]{1,0:T(8,128)(2,1)S(1)}, bf16[1024,1024]{1,0:T(8,128)(2,1)}, u32[]{:S(2)}) copy-start(bf16[1024,1024]{1,0:T(8,128)(2,1)} %all-gather.17.cloned.1.call-done) | copy-start | bytes 6291460
  544.6 15.4 %copy-start.49 = (bf16[1152]{0:T(1024)(128)(2,1)S(1)}, bf16[1152]{0:T(1024)(128)(2,1)}, u32[]{:S(2)}) copy-start(bf16[1152]{0:T(1024)(128)(2,1)} %pad.23.clone) | copy-start | bytes 6916
  567.0 140.3 %all-reduce.8.cloned.1.call-start = ((), (), s32[]{:S(2)}) async-start(), calls=%async_computation.21 | async-start | bytes 2097152 | tf_op jit(solution)/shard_map/psum | solution.py:320
  569.4 16.2 %copy-start.54 = (bf16[1024,1024]{1,0:T(8,128)(2,1)S(1)}, bf16[1024,1024]{1,0:T(8,128)(2,1)}, u32[]{:S(2)}) copy-start(bf16[1024,1024]{1,0:T(8,128)(2,1)} %all-gather.15.cloned.1.call-done) | copy-start | bytes 6291460
  614.7 50.6 %copy-start.29 = (f32[512,32]{0,1:T(8,128)S(1)}, f32[512,32]{0,1:T(8,128)}, u32[]{:S(2)}) copy-start(f32[512,32]{0,1:T(8,128)} %copy-done.28) | copy-start | bytes 196612
  629.6 39.3 %copy-start.9 = (bf16[4,1024,64]{1,2,0:T(8,128)(2,1)S(1)}, bf16[4,1024,64]{1,2,0:T(8,128)(2,1)}, u32[]{:S(2)}) copy-start(bf16[4,1024,64]{1,2,0:T(8,128)(2,1)} %copy-done.8) | copy-start | bytes 1572868
  666.1 2.7 copy-start.50
  668.8 38.6 %copy-start.1 = (bf16[1,512,1024]{1,2,0:T(8,128)(2,1)S(1)}, bf16[1,512,1024]{1,2,0:T(8,128)(2,1)}, u32[]{:S(2)}) copy-start(bf16[1,512,1024]{1,2,0:T(8,128)(2,1)} %copy-done) | copy-start | bytes 3145732
  668.8 38.6 %copy-start.4 = (bf16[512,1024]{0,1:T(8,128)(2,1)S(1)}, bf16[512,1024]{0,1:T(8,128)(2,1)}, u32[]{:S(2)}) copy-start(bf16[512,1024]{0,1:T(8,128)(2,1)} %all-reduce.6.cloned.1.call-done) | copy-start | bytes 3145732
  668.8 38.6 %copy-start.40 = (f32[1024,1]{0,1:T(1,128)S(1)}, f32[1024,1]{0,1:T(1,128)}, u32[]{:S(2)}) copy-start(f32[1024,1]{0,1:T(1,128)} %copy-done.39) | copy-start | bytes 12292
  668.8 38.6 %copy-start.44 = (f32[512]{0:T(512)S(1)}, f32[512]{0:T(512)}, u32[]{:S(2)}) copy-start(f32[512]{0:T(512)} %copy-done.43) | copy-start | bytes 6148
  668.8 100.7 %reduce-scatter.14.cloned.1.call-start = ((), (), s32[]{:S(2)}) async-start(), calls=%async_computation.22 | async-start | bytes 1572864 | tf_op jit(solution)/shard_map/reduce_scatter | solution.py:368
  707.4 3.0 copy-start.17
  707.4 3.0 copy-start.19
  710.4 3.2 copy-start.51
  710.4 4.7 copy-start.36
  710.4 4.7 copy-start.38
  710.4 4.7 copy-start.46
  749.1 112.4 %reduce-scatter.12.cloned.1.call-start = ((), (), s32[]{:S(2)}) async-start(), calls=%async_computation.20 | async-start | bytes 9437184 | tf_op jit(solution)/shard_map/reduce_scatter | solution.py:311
  749.7 144.9 %reduce-scatter.16.cloned.1.call-start = ((), (), s32[]{:S(2)}) async-start(), calls=%async_computation.24 | async-start | bytes 3145728 | tf_op jit(solution)/shard_map/reduce_scatter | solution.py:99
  750.4 178.7 %reduce-scatter.18.cloned.1.call-start = ((), (), s32[]{:S(2)}) async-start(), calls=%async_computation.26 | async-start | bytes 3145728 | tf_op jit(solution)/shard_map/reduce_scatter | solution.py:99
  751.0 212.7 %reduce-scatter.20.cloned.1.call-start = ((), (), s32[]{:S(2)}) async-start(), calls=%async_computation.28 | async-start | bytes 3145728 | tf_op jit(solution)/shard_map/reduce_scatter | solution.py:99
  751.6 278.1 %all-reduce.12.cloned.1.call-start = ((), (), s32[]{:S(2)}) async-start(), calls=%async_computation.33 | async-start | bytes 4194304 | tf_op jit(solution)/shard_map/psum | solution.py:327
  751.7 2.4 copy-start.27
  753.8 2.5 copy-start.15
  769.6 3.8 copy-start.16
  861.5 202.8 %all-gather.23.cloned.1.call-start = ((), (), s32[]{:S(2)}) async-start(), calls=%async_computation.25 | async-start | bytes 3145728 | tf_op jit(solution)/shard_map/all_gather | solution.py:106
  925.9 173.0 %all-gather.25.cloned.1.call-start = ((), (), s32[]{:S(2)}) async-start(), calls=%async_computation.27 | async-start | bytes 3145728 | tf_op jit(solution)/shard_map/all_gather | solution.py:106
  960.7 173.0 %all-gather.27.cloned.1.call-start = ((), (), s32[]{:S(2)}) async-start(), calls=%async_computation.29 | async-start | bytes 3145728 | tf_op jit(solution)/shard_map/all_gather | solution.py:106
  997.4 181.2 %reduce-scatter.22.cloned.1.call-start = ((), (), s32[]{:S(2)}) async-start(), calls=%async_computation.32 | async-start | bytes 3833856
  1000.4 4.3 copy-start.22
  1000.4 4.3 copy-start.33
  1000.4 4.3 copy-start.42
  1000.4 4.3 copy-start.48
  1054.8 151.9 %all-reduce.10.cloned.1.call-start = ((), (), s32[]{:S(2)}) async-start(), calls=%async_computation.23 | async-start | bytes 786432 | tf_op jit(solution)/shard_map/psum | solution.py:420
  1138.1 42.5 %copy-start.18 = (bf16[512,1024]{0,1:T(8,128)(2,1)S(1)}, bf16[512,1024]{0,1:T(8,128)(2,1)}, u32[]{:S(2)}) copy-start(bf16[512,1024]{0,1:T(8,128)(2,1)} %all-reduce.8.cloned.1.call-done) | copy-start | bytes 3145732
  1143.8 36.8 %copy-start.5 = (bf16[512,1024]{0,1:T(8,128)(2,1)S(1)}, bf16[512,1024]{0,1:T(8,128)(2,1)}, u32[]{:S(2)}) copy-start(bf16[512,1024]{0,1:T(8,128)(2,1)} %all-reduce.6.cloned.1.call-done) | copy-start | bytes 3145732
  1184.8 3.0 copy-start.20
  1206.8 4.2 copy-start.23
  (28 other events, 39.4 us)
Sparse Core Ops, SparseCore 0:
  20.3 46.1 all-gather.12
  72.0 19.5 all-gather.28
  132.4 40.0 all-reduce.5
  174.6 33.1 all-gather.16
  209.8 33.1 all-gather.18
  244.4 33.1 all-gather.14
  279.2 82.0 all-gather.30
  363.0 80.5 all-gather.20
  567.2 98.0 reduce-scatter.9
  669.0 38.3 all-reduce.7
  749.2 20.3 reduce-scatter.13
  771.8 89.5 reduce-scatter.11
  864.4 30.1 reduce-scatter.15
  897.3 31.8 reduce-scatter.17
  931.9 31.8 reduce-scatter.19
  966.5 63.1 all-reduce.11
  1031.2 33.1 all-gather.22
  1065.8 33.1 all-gather.24
  1100.6 33.1 all-gather.26
  1136.0 42.5 reduce-scatter.21
  1181.0 24.4 all-reduce.9
